TPU v7x, 128 devices: a whole 4x4x4 slice. The times are simulated.
128 devices in a mesh: elem: 32 (over y, x, core), blk: 4 (over z).
Axes of the slice: x: 4, y: 4, z: 4, core: 2. Of those that a mesh axis runs over, the one named last changes fastest.
Arguments:
- state: float32 [2048, 128, 4, 128], P('elem', 'blk'), may hold values from -6 to 6
- wind_x: float32 [2048, 128, 128], P('elem', 'blk'), may hold values from -6 to 6
- wind_y: float32 [2048, 128, 128], P('elem', 'blk'), may hold values from -6 to 6
- mixing: float32 [128, 128], replicated, may hold values from -1 to 0.92
- triggers: int32 [2048, 128], P('elem', 'blk'), may hold values 0 or 1
- group_costs: int32 [16384], P(('elem', 'blk')), may hold values from 1 to 64, as said below
- destinations: int32 [16384], P(('elem', 'blk')), may hold values from 0 to 127, as said below
Outputs:
- new_state: float32 [2048, 128, 4, 128], P('elem', 'blk')
- precipitation: float32 [262144], P(('elem', 'blk'))
Inputs may be any that keep to these rules, and one draw needn't show every extreme that they name: `destinations`: every device is the destination of exactly 128 groups, at most 2 groups of one device go to one device, and some pair of devices reaches 2. `group_costs`: some group reaches 64.
All inputs are finite; a program needn't handle non-finite values. No bound on the sum of `triggers` on one device may be relied on, other than what follows from the above.
Results may differ from a plain program's by a relative error of at most 0.0001.
Values sent between devices are 32-bit elements; how exact they have to be, the bound alone decides.
No kernel may reach another device: no remote copies, remote signals or barrier semaphores. Data moves between devices by JAX's collectives and lax.ppermute only.
A program may use at most 128 MiB of HBM per device.

v0:
```python
import functools

import jax
import jax.numpy as jnp
import numpy as np
from jax import lax
from jax.experimental import pallas as pl
from jax.experimental.pallas import tpu as pltpu
from jax.sharding import PartitionSpec as P

NP = 4
NT = 4
LEV = 128
GROUP_COLS = 16
MAXC = 64
LIMIT = 1.0e3
F32 = jnp.float32
BF16 = jnp.bfloat16
MIB = 1024 * 1024


def gll_derivative():
    nodes = np.array([-1.0, -1.0 / np.sqrt(5.0), 1.0 / np.sqrt(5.0), 1.0])
    legendre = (5.0 * nodes * nodes * nodes - 3.0 * nodes) / 2.0
    derivative = np.zeros((4, 4))
    for a in range(4):
        for b in range(4):
            if a != b:
                derivative[a, b] = legendre[a] / (legendre[b] * (nodes[a] - nodes[b]))
    derivative[0, 0] = -3.0
    derivative[3, 3] = 3.0
    return derivative


def split2(x):
    high = x.astype(BF16)
    return high, (x - high.astype(F32)).astype(BF16)


def split3(x):
    high = x.astype(BF16)
    rest = x - high.astype(F32)
    mid = rest.astype(BF16)
    return high, mid, (rest - mid.astype(F32)).astype(BF16)


def mm(a, b):
    return jnp.dot(a, b, preferred_element_type=F32)


def exact_pick(onehot, values):
    high, mid, low = split3(values)
    return mm(onehot, high) + mm(onehot, mid) + mm(onehot, low)


def weights(high, mid, low):
    pair = jnp.concatenate([high, mid], axis=1)
    return jnp.concatenate([pair, pair], axis=0), jnp.concatenate([low, high], axis=0)


def precise(high, mid, low, first, second):
    one = mm(jnp.concatenate([high, mid], axis=1), first)
    two = mm(jnp.concatenate([high, low], axis=1), second)
    return one[:, :LEV] + (one[:, LEV:] + two)


def repeated(start, cost, first_ref, second_ref):
    return lax.fori_loop(0, cost, lambda i, c: precise(*split3(c), first_ref[...], second_ref[...]), start)


def iota(shape, dim):
    return lax.broadcasted_iota(jnp.int32, shape, dim)


def gains_kernel(mixing_ref, dest_ref, trig_ref, gain_ref, onehot_ref, mask_ref, first_ref, second_ref, bad_ref, sums):
    square = mixing_ref[...]
    worst = jnp.max(jnp.abs(square))
    first_ref[...], second_ref[...] = weights(*split3(square.T))
    sums[0:8] = jnp.broadcast_to(jnp.sum(square, axis=0, keepdims=True), (8, LEV))
    for k in (1, 2, 4, 8, 16, 32):
        parts = split3(square)
        pair = weights(*parts)
        rows = max(k, 8)
        grown = precise(*split3(sums[0:rows]), *pair)
        if k < 8:
            pick = iota((8, LEV), 0)
            merged = sums[0:8]
            for j in range(k):
                merged = jnp.where(pick == j + k, grown[j:j + 1], merged)
            sums[0:8] = merged
        else:
            sums[k:2 * k] = grown
        if k < 32:
            square = precise(*parts, *pair)
            worst = jnp.maximum(worst, jnp.max(jnp.abs(square)))
    gain_ref[...] = 1.0 - sums[...]
    bad_ref[0] = jnp.where(worst <= LIMIT, 0, 1).astype(jnp.int32)

    groups = dest_ref.shape[1]
    shape = (groups, groups)
    dest_row = jnp.broadcast_to(dest_ref[...], shape)
    diagonal = iota(shape, 0) == iota(shape, 1)
    dest_col = jnp.sum(jnp.where(diagonal, dest_row, 0), axis=1, keepdims=True)
    earlier = (dest_col == dest_row) & (iota(shape, 0) < iota(shape, 1))
    within = jnp.sum(jnp.where(earlier, 1, 0), axis=0, keepdims=True)
    at = dest_row == iota(shape, 0)
    onehot_ref[0] = jnp.where(at & (within == 0), 1.0, 0.0).astype(BF16)
    onehot_ref[1] = jnp.where(at & (within == 1), 1.0, 0.0).astype(BF16)

    px, py = trig_ref.shape
    rows = py * NT
    trig = jnp.concatenate([trig_ref[...].astype(F32), jnp.zeros((LEV - px, py), F32)], axis=0).T
    spread = jnp.where(iota((rows, py), 0) // NT == iota((rows, py), 1), 1.0, 0.0).astype(BF16)
    mask_ref[...] = mm(spread, trig.astype(BF16))


def half_coefs(first, second):
    return jnp.where(iota((8, LEV), 0) < 4, F32(first), F32(second))


def derivative_tables():
    deriv = -0.05 * gll_derivative()
    g = [[float(np.float32(deriv[a, b])) for b in range(4)] for a in range(4)]
    low = [half_coefs(g[0][0], g[1][1]), half_coefs(g[0][1], g[1][0]), half_coefs(g[0][2], g[1][3]), half_coefs(g[0][3], g[1][2])]
    high = [half_coefs(g[2][0], g[3][1]), half_coefs(g[2][1], g[3][0]), half_coefs(g[2][2], g[3][3]), half_coefs(g[2][3], g[3][2])]
    return g, low, high


def tendency(k, points, load, load_x, load_y, store):
    g, low, high = derivative_tables()
    lower = iota((8, LEV), 0) < 4
    v = [[load(a, 16 * k + 8 * h) for h in range(2)] for a in range(NP)]
    for a in points:
        r = [pltpu.roll(v[a][h], 4, axis=0) for h in range(2)]
        for h, coefs in ((0, low), (1, high)):
            along_y = (coefs[0] * v[a][0] + coefs[1] * r[0]) + (coefs[2] * v[a][1] + coefs[3] * r[1])
            along_x = (g[a][0] * v[0][h] + g[a][1] * v[1][h]) + (g[a][2] * v[2][h] + g[a][3] * v[3][h])
            y = 4 * k + 2 * h
            wx = jnp.where(lower, load_x(a, y), load_x(a, y + 1))
            wy = jnp.where(lower, load_y(a, y), load_y(a, y + 1))
            store(a, 16 * k + 8 * h, wx * along_x + wy * along_y)


def sides_kernel(par_ref, low_ref, high_ref, low_x_ref, high_x_ref, low_y_ref, high_y_ref, send_a_ref, send_b_ref, first_ref, final_ref):
    even = par_ref[0] == 0
    for k in range(low_ref.shape[1] // 16):
        for ref, x_ref, y_ref, out_ref, at in ((low_ref, low_x_ref, low_y_ref, first_ref, 0), (high_ref, high_x_ref, high_y_ref, final_ref, NP - 1)):
            def load(a, i, ref=ref):
                return ref[a, i:i + 8, :]

            def store(a, i, value, out_ref=out_ref):
                out_ref[i:i + 8, :] = value

            tendency(k, (at,), load, lambda a, y, ref=x_ref: ref[0, y:y + 1, :], lambda a, y, ref=y_ref: ref[0, y:y + 1, :], store)
    first, final = first_ref[...], final_ref[...]
    send_a_ref[...] = jnp.where(even, final, first)
    send_b_ref[...] = jnp.where(even, first, final)


def smooth_rows(v, up, down):
    m0, n0 = half_coefs(0.5, 1.0), half_coefs(0.5, 0.0)
    m1, n1 = half_coefs(1.0, 0.5), half_coefs(0.0, 0.5)
    r = [pltpu.roll(piece, 4, axis=0) for piece in v]
    out = []
    for i in range(len(v)):
        if i % 2 == 0:
            other = r[i - 1] if i else up
            out.append(m0 * v[i] if other is None else m0 * v[i] + n0 * other)
        else:
            other = r[i + 1] if i < len(v) - 1 else down
            out.append(m1 * v[i] if other is None else m1 * v[i] + n1 * other)
    return out


def local_kernel(state_hbm, wx_hbm, wy_hbm, adv_hbm, tracer_ref, edge_ref, state, wx, wy, tend, adv, sems, out_sems):
    elements = state.shape[0] // NP
    rows = state.shape[1]
    lower = iota((8, LEV), 0) < 4

    def piece(e):
        return pl.ds(e * NP, NP)

    def copies(e):
        return [pltpu.make_async_copy(src.at[piece(e)], dst.at[piece(e)], sems.at[i, e]) for i, (src, dst) in enumerate(((state_hbm, state), (wx_hbm, wx), (wy_hbm, wy)))]

    def out_copy(e):
        return pltpu.make_async_copy(adv.at[piece(e)], adv_hbm.at[piece(e)], out_sems.at[e])

    for e in range(elements):
        for copy in copies(e):
            copy.start()

    def differentiate(e):
        for copy in copies(e):
            copy.wait()

        def load(a, i):
            return state[e * NP + a, i:i + 8, :]

        def store(a, i, value):
            tend[e * NP + a, i:i + 8, :] = value

        for k in range(rows // 16):
            tendency(k, range(NP), load, lambda a, y: wx[e * NP + a, y:y + 1, :], lambda a, y: wy[e * NP + a, y:y + 1, :], store)

    def finish(e):
        for a in range(NP):
            x = e * NP + a
            v = [tend[x, 8 * i:8 * i + 8, :] for i in range(rows // 8)]
            if a == 0:
                left = jnp.maximum(x - 1, 0)
                share = jnp.where(e > 0, 0.5, 0.0).astype(F32)
                v = [0.5 * v[i] + share * tend[left, 8 * i:8 * i + 8, :] for i in range(rows // 8)]
            if a == NP - 1:
                right = jnp.minimum(x + 1, elements * NP - 1)
                share = jnp.where(e < elements - 1, 0.5, 0.0).astype(F32)
                v = [0.5 * v[i] + share * tend[right, 8 * i:8 * i + 8, :] for i in range(rows // 8)]
            edge_ref[x] = jnp.where(lower, v[0], v[-1])
            for i, value in enumerate(smooth_rows(v, None, None)):
                adv[x, 8 * i:8 * i + 8, :] = state[x, 8 * i:8 * i + 8, :] + value
            tracer_ref[x] = adv[x, pl.ds(1, rows // NT, stride=NT), :]
        out_copy(e).start()

    differentiate(0)

    def step(e, carry):
        differentiate(e)
        finish(e - 1)
        return carry

    lax.fori_loop(1, elements, step, 0)
    finish(elements - 1)
    for e in range(elements):
        out_copy(e).wait()


def edge_kernel(par_ref, edge_ref, got_a_ref, got_b_ref, send_c_ref, send_d_ref):
    even = par_ref[0] == 0
    even_y = par_ref[1] == 0
    px = edge_ref.shape[0]
    rows = got_a_ref.shape[0]
    lower = iota((8, LEV), 0) < 4
    before = jnp.where(even, got_b_ref[...], got_a_ref[...])
    after = jnp.where(even, got_a_ref[...], got_b_ref[...])
    for x in range(px):
        both = edge_ref[x]
        if x == 0:
            both = both + 0.5 * jnp.where(lower, before[0:8], before[rows - 8:rows])
        if x == px - 1:
            both = both + 0.5 * jnp.where(lower, after[0:8], after[rows - 8:rows])
        send_c_ref[x] = jnp.where(even_y, both[4:8], both[0:4])
        send_d_ref[x] = jnp.where(even_y, both[0:4], both[4:8])


def side_shares(even, got_a_ref, got_b_ref, rows):
    before = [0.5 * jnp.where(even, got_b_ref[i:i + 8, :], got_a_ref[i:i + 8, :]) for i in range(0, rows, 8)]
    after = [0.5 * jnp.where(even, got_a_ref[i:i + 8, :], got_b_ref[i:i + 8, :]) for i in range(0, rows, 8)]
    return smooth_rows(before, None, None), smooth_rows(after, None, None)


def rain_kernel(par_ref, cost_ref, bad_ref, tracer_ref, got_a_ref, got_b_ref, got_c_ref, got_d_ref, mask_ref, gain_ref, onehot_ref, first_ref, second_ref, out_ref, rain_ref, side_ref, z_ref):
    px, py, _ = tracer_ref.shape
    half = py // 2
    rows = py * NT
    even_y = par_ref[1] == 0
    for s, side in enumerate(side_shares(par_ref[0] == 0, got_a_ref, got_b_ref, rows)):
        for i, value in enumerate(side):
            side_ref[s, 8 * i:8 * i + 8, :] = value
    at_first = iota((half, LEV), 0) == 0
    at_final = iota((half, LEV), 0) == half - 1

    def advanced(x):
        up = 0.5 * jnp.where(even_y, got_d_ref[x, 1:2, :], got_c_ref[x, 1:2, :])
        down = 0.5 * jnp.where(even_y, got_c_ref[x, 1:2, :], got_d_ref[x, 1:2, :])
        low = tracer_ref[x, 0:half, :] + jnp.where(at_first, up, 0.0)
        high = tracer_ref[x, half:py, :] + jnp.where(at_final, down, 0.0)
        if isinstance(x, int):
            extra = side_ref[0 if x == 0 else 1, pl.ds(1, py, stride=NT), :]
            return low + extra[0:half], high + extra[half:py]
        return low, high

    ones = jnp.ones((2 * LEV, LEV), BF16)
    place = (iota((half, LEV), 1) < 2 * half) & (iota((half, LEV), 1) % half == iota((half, LEV), 0))

    def weigh(x, part, h):
        return part * gain_ref[pl.ds(cost_ref[2 * x + h] - 1, 1), :]

    def step_by_step(x, part, h):
        return part - repeated(part, cost_ref[2 * x + h], first_ref, second_ref)

    def fill(rule):
        def one(x):
            for h, part in enumerate(advanced(x)):
                z_ref[x, half * h:half * h + half, :] = rule(x, part, h)

        one(0)
        one(px - 1)

        def step(x, carry):
            one(x)
            return carry

        lax.fori_loop(1, px - 1, step, 0, unroll=2)

    @pl.when(bad_ref[0] == 0)
    def _():
        fill(weigh)

    @pl.when(bad_ref[0] != 0)
    def _():
        fill(step_by_step)

    def total(x, carry):
        high, low = split2(z_ref[x])
        sums = mm(jnp.concatenate([high, low], axis=1), ones) * 0.125
        for h in range(2):
            spread = jnp.where(place, sums[half * h:half * h + half], 0.0)
            rain_ref[pl.ds(2 * x + h, 1), :] = jnp.sum(spread, axis=0, keepdims=True)
        return carry

    lax.fori_loop(0, px, total, 0, unroll=4)
    lane = iota(out_ref.shape, 1)
    values = jnp.where(lane == 2 * half, 1.0, jnp.where(mask_ref[...] > 0, rain_ref[...], 0.0))
    first = exact_pick(onehot_ref[0], values)
    second = exact_pick(onehot_ref[1], values)
    out_ref[...] = jnp.where(lane < half, first, jnp.where(lane < 2 * half, second, first + second))


def mix_kernel(par_ref, cost_ref, bad_ref, mixing_ref, mask_ref, got_a_ref, got_b_ref, got_c_ref, got_d_ref, first_ref, second_ref, adv_hbm, new_hbm, adv, new, powers, sems, out_sems):
    px, rows, _ = adv.shape
    half = rows // 2
    elements = px // NP
    even_y = par_ref[1] == 0
    lower = iota((8, LEV), 0) < 4

    def piece(e):
        return pl.ds(e * NP, NP)

    def in_copy(e):
        return pltpu.make_async_copy(adv_hbm.at[piece(e)], adv.at[piece(e)], sems.at[e])

    def out_copy(e):
        return pltpu.make_async_copy(new.at[piece(e)], new_hbm.at[piece(e)], out_sems.at[e])

    for e in range(elements):
        in_copy(e).start()

    @pl.when(bad_ref[0] == 0)
    def _():
        powers[0] = jnp.concatenate(split3(mixing_ref[...].T), axis=1)
        for k in (1, 2, 4, 8, 16, 32):
            def part(j):
                return powers[j, :, 0:LEV], powers[j, :, LEV:2 * LEV], powers[j, :, 2 * LEV:3 * LEV]

            first, second = weights(*part(k - 1))

            def step(j, carry):
                powers[j + k] = jnp.concatenate(split3(precise(*part(j), first, second)), axis=1)
                return carry

            lax.fori_loop(0, k, step, 0, unroll=min(k, 4))

    shares = side_shares(par_ref[0] == 0, got_a_ref, got_b_ref, rows)
    for e, x, share in ((0, 0, shares[0]), (elements - 1, px - 1, shares[1])):
        in_copy(e).wait()
        for i in range(rows // 8):
            adv[x, 8 * i:8 * i + 8, :] = adv[x, 8 * i:8 * i + 8, :] + share[i]

    def element(e, carry):
        @pl.when((e > 0) & (e < elements - 1))
        def _():
            in_copy(e).wait()

        rolled = pltpu.roll(mask_ref[...], lax.rem(LEV - e * NP, LEV), axis=1)
        for a in range(NP):
            x = e * NP + a
            up = 0.5 * jnp.where(even_y, got_d_ref[x], got_c_ref[x])
            down = 0.5 * jnp.where(even_y, got_c_ref[x], got_d_ref[x])
            adv[x, 0:4, :] = adv[x, 0:4, :] + up
            adv[x, rows - 4:rows, :] = adv[x, rows - 4:rows, :] + down
            mask = jnp.broadcast_to(rolled[:, a:a + 1], (rows, LEV))

            @pl.when(bad_ref[0] == 0)
            def _():
                for h in range(2):
                    part = slice(half * h, half * h + half)
                    start = adv[x, part, :]
                    high, low = split2(start)
                    both = mm(jnp.concatenate([high, low], axis=0), powers[cost_ref[2 * x + h] - 1, :, 0:2 * LEV])
                    done = (both[:half, :LEV] + both[half:, :LEV]) + (both[:half, LEV:] + both[half:, LEV:])
                    new[x, part, :] = jnp.where(mask[part] > 0.5, done, start)

            @pl.when(bad_ref[0] != 0)
            def _():
                for h in range(2):
                    part = slice(half * h, half * h + half)
                    start = adv[x, part, :]
                    done = repeated(start, cost_ref[2 * x + h], first_ref, second_ref)
                    new[x, part, :] = jnp.where(mask[part] > 0.5, done, start)

        out_copy(e).start()
        return carry

    lax.fori_loop(0, elements, element, 0)
    for e in range(elements):
        out_copy(e).wait()


def gather_kernel(got_ref, rain_ref):
    got = got_ref[...]
    size = got.shape
    half = GROUP_COLS
    count_col = jnp.sum(jnp.where(iota(size, 1) == 2 * half, got, 0.0), axis=1, keepdims=True)
    earlier = jnp.where(iota(size, 0) < iota(size, 1), count_col, 0.0)
    start = jnp.sum(earlier, axis=0, keepdims=True).astype(jnp.int32)
    count = jnp.sum(jnp.where(iota(size, 0) == iota(size, 1), count_col, 0.0), axis=0, keepdims=True).astype(jnp.int32)
    per = LEV // half
    rows = size[0] // per
    slot = (iota(size, 0) % rows) * per + iota(size, 0) // rows
    pick0 = jnp.where((slot == start) & (count > 0), 1.0, 0.0).astype(BF16)
    pick1 = jnp.where((slot == start + 1) & (count > 1), 1.0, 0.0).astype(BF16)
    tile0 = jnp.where(iota(size, 0) == iota(size, 1) % half, 1.0, 0.0).astype(BF16)
    tile1 = jnp.where(iota(size, 0) == iota(size, 1) % half + half, 1.0, 0.0).astype(BF16)

    def tiled(tile):
        high, mid, low = split3(got)
        return mm(high, tile).astype(BF16), mm(mid, tile).astype(BF16), mm(low, tile).astype(BF16)

    total = jnp.zeros(size, F32)
    for pick, tile in ((pick0, tile0), (pick1, tile1)):
        high, mid, low = tiled(tile)
        total = total + ((mm(pick, high) + mm(pick, mid)) + mm(pick, low))
    lane = iota((rows, LEV), 1)
    out = jnp.zeros((rows, LEV), F32)
    for q in range(per):
        out = jnp.where(lane // half == q, total[q * rows:(q + 1) * rows], out)
    rain_ref[...] = out


SMEM = pl.BlockSpec(memory_space=pltpu.SMEM)
VMEM = pl.BlockSpec(memory_space=pltpu.VMEM)
HBM = pl.BlockSpec(memory_space=pltpu.HBM)


def params(mib):
    return pltpu.CompilerParams(vmem_limit_bytes=mib * MIB)


def cost(flops, moved):
    return pl.CostEstimate(flops=flops, bytes_accessed=moved, transcendentals=0)


def body(state, wind_x, wind_y, mixing, triggers, group_costs, destinations):
    px, py, nt, lev = state.shape
    rows = py * nt
    groups = group_costs.shape[0]
    elements = px // NP
    n_elem, n_blk = lax.axis_size("elem"), lax.axis_size("blk")
    slabs = state.reshape(px, rows, lev)
    parity = jnp.stack([lax.axis_index("elem") % 2, lax.axis_index("blk") % 2]).astype(jnp.int32)
    lanes = jnp.pad(jnp.tile(triggers.reshape(groups, GROUP_COLS), (1, 2)), ((0, 0), (0, lev - 2 * GROUP_COLS)))

    def struct(*shape, dtype=F32):
        return jax.ShapeDtypeStruct(shape, dtype)

    def block(shape, *at):
        return pl.BlockSpec(shape, lambda i: at)

    send_a, send_b = pl.pallas_call(
        sides_kernel,
        grid=(1,),
        out_shape=(struct(rows, lev),) * 2,
        in_specs=[
            SMEM,
            block((NP, rows, lev), 0, 0, 0),
            block((NP, rows, lev), elements - 1, 0, 0),
            block((1, py, lev), 0, 0, 0),
            block((1, py, lev), px - 1, 0, 0),
            block((1, py, lev), 0, 0, 0),
            block((1, py, lev), px - 1, 0, 0),
        ],
        out_specs=(block((rows, lev), 0, 0),) * 2,
        scratch_shapes=[pltpu.VMEM((rows, lev), F32)] * 2,
        compiler_params=params(60),
        cost_estimate=cost(2 * MIB, MIB),
        name="sides",
    )(parity, slabs, slabs, wind_x, wind_x, wind_y, wind_y)

    pair_a = [(i, i ^ 1) for i in range(n_elem)]
    pair_b = [(i, (i - 1 if i % 2 == 0 else i + 1) % n_elem) for i in range(n_elem)]
    pair_c = [(j, j ^ 1) for j in range(n_blk)]
    pair_d = [(j, (j - 1 if j % 2 == 0 else j + 1) % n_blk) for j in range(n_blk)]
    got_a = lax.ppermute(send_a, "elem", pair_a)
    got_b = lax.ppermute(send_b, "elem", pair_b)

    local, tracer, edges = pl.pallas_call(
        local_kernel,
        out_shape=(struct(px, rows, lev), struct(px, py, lev), struct(px, 8, lev)),
        in_specs=[HBM, HBM, HBM],
        out_specs=(HBM, VMEM, VMEM),
        scratch_shapes=[
            pltpu.VMEM((px, rows, lev), F32),
            pltpu.VMEM((px, py, lev), F32),
            pltpu.VMEM((px, py, lev), F32),
            pltpu.VMEM((px, rows, lev), F32),
            pltpu.VMEM((px, rows, lev), F32),
            pltpu.SemaphoreType.DMA((3, elements)),
            pltpu.SemaphoreType.DMA((elements,)),
        ],
        compiler_params=params(60),
        cost_estimate=cost(64 * MIB, 12 * MIB),
        name="local",
    )(slabs, wind_x, wind_y)

    send_c, send_d = pl.pallas_call(
        edge_kernel,
        out_shape=(struct(px, nt, lev),) * 2,
        in_specs=[SMEM, VMEM, VMEM, VMEM],
        out_specs=(VMEM, VMEM),
        compiler_params=params(8),
        cost_estimate=cost(MIB, MIB),
        name="edges",
    )(parity, edges, got_a, got_b)
    got_c = lax.ppermute(send_c, "blk", pair_c)
    got_d = lax.ppermute(send_d, "blk", pair_d)

    gains, onehots, mask, first, second, bad = pl.pallas_call(
        gains_kernel,
        out_shape=(
            struct(MAXC, lev),
            struct(2, groups, groups, dtype=BF16),
            struct(rows, lev),
            struct(2 * lev, 2 * lev, dtype=BF16),
            struct(2 * lev, lev, dtype=BF16),
            struct(1, dtype=jnp.int32),
        ),
        in_specs=[VMEM, VMEM, VMEM],
        out_specs=(VMEM, VMEM, VMEM, VMEM, VMEM, SMEM),
        scratch_shapes=[pltpu.VMEM((MAXC, lev), F32)],
        compiler_params=params(8),
        cost_estimate=cost(512 * MIB, MIB),
        name="gains",
    )(mixing, destinations.reshape(1, groups), triggers)

    outgoing = pl.pallas_call(
        rain_kernel,
        out_shape=struct(groups, lev),
        in_specs=[SMEM, SMEM, SMEM] + [VMEM] * 10,
        out_specs=VMEM,
        scratch_shapes=[pltpu.VMEM((groups, lev), F32), pltpu.VMEM((2, rows, lev), F32), pltpu.VMEM((px, py, lev), F32)],
        compiler_params=params(12),
        cost_estimate=cost(64 * MIB, 2 * MIB),
        name="rain",
    )(parity, group_costs, bad, tracer, got_a, got_b, got_c, got_d, lanes, gains, onehots, first, second)

    incoming = lax.all_to_all(outgoing, ("elem", "blk"), split_axis=0, concat_axis=0, tiled=True)

    new = pl.pallas_call(
        mix_kernel,
        out_shape=struct(px, rows, lev),
        in_specs=[SMEM, SMEM, SMEM] + [VMEM] * 8 + [HBM],
        out_specs=HBM,
        scratch_shapes=[
            pltpu.VMEM((px, rows, lev), F32),
            pltpu.VMEM((px, rows, lev), F32),
            pltpu.VMEM((MAXC, lev, 3 * lev), BF16),
            pltpu.SemaphoreType.DMA((elements,)),
            pltpu.SemaphoreType.DMA((elements,)),
        ],
        compiler_params=params(60),
        cost_estimate=cost(4096 * MIB, 10 * MIB),
        name="mix",
    )(parity, group_costs, bad, mixing, mask, got_a, got_b, got_c, got_d, first, second, local)

    rain = pl.pallas_call(
        gather_kernel,
        out_shape=struct(groups * GROUP_COLS // lev, lev),
        in_specs=[VMEM],
        out_specs=VMEM,
        compiler_params=params(8),
        cost_estimate=cost(MIB, MIB),
        name="gather",
    )(incoming)
    return new.reshape(state.shape), rain.reshape(-1)


def solution(mesh):
    return jax.shard_map(
        body,
        mesh=mesh,
        in_specs=(
            P("elem", "blk", None, None),
            P("elem", "blk", None),
            P("elem", "blk", None),
            P(),
            P("elem", "blk"),
            P(("elem", "blk")),
            P(("elem", "blk")),
        ),
        out_specs=(P("elem", "blk", None, None), P(("elem", "blk"))),
        check_vma=False,
    )
```

profile of v0, /device:TPU:1, one launch (start us, length us, event | category | flops | bytes accessed | tf_op | source)
XLA Modules:
  0.0 59.9 jit_solution(15121526928617754393)
XLA Ops:
  0.6 0.6 %pad_add_fusion.par_ref = s32[2]{0:T(128)} fusion(s32[1]{0:T(128)} %bitcast.1, s32[1]{0:T(128)} %bitcast), kind=kLoop, calls=%fused_computation | loop fusion | flops 2 | bytes 16 | tf_op jit(solution)/shard_map/stack | solution.py:460
  1.3 1.8 %sides.1 = (f32[128,128]{1,0:T(8,128)}, f32[128,128]{1,0:T(8,128)}) custom-call(s32[2]{0:T(128)} %pad_add_fusion.par_ref, f32[64,128,128]{2,1,0:T(8,128)} %bitcast.13, f32[64,128,128]{2,1,0:T(8,128)} %bitcast.14, f32[64,32,128]{2,1,0:T(8,128)} %wx_hbm.1, f32[64,32,128]{2,1,0:T(8,128)} %wx_hbm.1, f32[64,32,128]{2,1,0:T(8,128)} %wy_hbm.1, f32[64,32,128]{2,1,0:T(8,128)} %wy_hbm.1), custom_call_target="tpu_custom_call" | custom-call | flops 2097152 | bytes 1048576 | tf_op jit(solution)/shard_map/sides/pallas_call | solution.py:469
  3.1 0.0 copy-start.11
  3.1 1.5 %collective-permute-start = (f32[128,128]{1,0:T(8,128)}, f32[128,128]{1,0:T(8,128)S(1)}, u32[]{:S(2)}, u32[]{:S(2)}) collective-permute-start(f32[128,128]{1,0:T(8,128)} %get-tuple-element.17), channel_id=1, source_target_pairs={{0,4},{4,0},{8,12},{12,8},{16,20},{20,16},{24,28},{28,24},{32,36},... | collective-permute-start | bytes 196616 | tf_op jit(solution)/shard_map/ppermute | solution.py:493
  4.6 1.3 %collective-permute-start.1 = (f32[128,128]{1,0:T(8,128)}, f32[128,128]{1,0:T(8,128)S(1)}, u32[]{:S(2)}, u32[]{:S(2)}) collective-permute-start(f32[128,128]{1,0:T(8,128)} %get-tuple-element.18), channel_id=1, source_target_pairs={{0,124},{4,8},{8,4},{12,16},{16,12},{20,24},{24,20},{28,32},{32,28... | collective-permute-start | bytes 196616 | tf_op jit(solution)/shard_map/ppermute | solution.py:494
  5.9 7.3 %local.1 = (f32[64,128,128]{2,1,0:T(8,128)}, f32[64,32,128]{2,1,0:T(8,128)}, f32[64,8,128]{2,1,0:T(8,128)}) custom-call(f32[64,128,128]{2,1,0:T(8,128)} %bitcast.15, f32[64,32,128]{2,1,0:T(8,128)} %wx_hbm.1, f32[64,32,128]{2,1,0:T(8,128)} %wy_hbm.1), custom_call_target="tpu_custom_call" | custom-call | flops 67108864 | bytes 12582912 | tf_op jit(solution)/shard_map/local/pallas_call | solution.py:496
  13.1 0.0 collective-permute-done.got_a_ref
  13.2 0.0 collective-permute-done.1.got_b_ref
  13.2 1.0 %copy-done.1 = f32[64,8,128]{2,1,0:T(8,128)S(1)} copy-done((f32[64,8,128]{2,1,0:T(8,128)S(1)}, f32[64,8,128]{2,1,0:T(8,128)}, u32[]{:S(2)}) %copy-start.1) | copy-done | bytes 262168
  14.2 0.6 edges.1
  14.8 1.7 %collective-permute-start.2 = (f32[64,4,128]{2,1,0:T(4,128)S(1)}, f32[64,4,128]{2,1,0:T(4,128)S(1)}, u32[]{:S(2)}, u32[]{:S(2)}) collective-permute-start(f32[64,4,128]{2,1,0:T(4,128)S(1)} %get-tuple-element.20), channel_id=1, source_target_pairs={{0,1},{1,0},{2,3},{3,2},{4,5},{5,4},{6,7},{7,6},{8,9},{9,8},{10,11... | collective-permute-start | bytes 393224 | tf_op jit(solution)/shard_map/ppermute | solution.py:524
  16.5 2.2 %collective-permute-start.3 = (f32[64,4,128]{2,1,0:T(4,128)S(1)}, f32[64,4,128]{2,1,0:T(4,128)S(1)}, u32[]{:S(2)}, u32[]{:S(2)}) collective-permute-start(f32[64,4,128]{2,1,0:T(4,128)S(1)} %get-tuple-element.21), channel_id=1, source_target_pairs={{0,3},{1,2},{2,1},{3,0},{4,7},{5,6},{6,5},{7,4},{8,11},{9,10},{10,... | collective-permute-start | bytes 393224 | tf_op jit(solution)/shard_map/ppermute | solution.py:525
  18.7 0.1 copy.14.trig_ref
  18.8 0.1 tile.10
  18.9 0.1 copy.16
  18.9 0.1 copy.17
  19.1 1.7 %gains.1 = (f32[64,128]{1,0:T(8,128)S(1)}, bf16[2,128,128]{2,1,0:T(8,128)(2,1)S(1)}, f32[128,128]{1,0:T(8,128)S(1)}, bf16[256,256]{1,0:T(8,128)(2,1)S(1)}, bf16[256,128]{1,0:T(8,128)(2,1)S(1)}, /*index=5*/s32[1]{0:T(128)}) custom-call(f32[128,128]{1,0:T(8,128)S(1)} %copy-done.10, s32[1,128]{1,0:T(1,128)S(1)} %bitcast.12, s32[64,32]{1,0:T(8,128)S(1)} %copy.14.trig_ref), custom_call_target="tpu_custom_call" | custom-call | flops 536870912 | bytes 1048576 | tf_op jit(solution)/shard_map/gains/pallas_call | solution.py:527
  20.8 0.0 collective-permute-done.2.got_c_ref
  20.8 0.7 %collective-permute-done.3.got_d_ref = f32[64,4,128]{2,1,0:T(4,128)S(1)} collective-permute-done((f32[64,4,128]{2,1,0:T(4,128)S(1)}, f32[64,4,128]{2,1,0:T(4,128)S(1)}, u32[]{:S(2)}, u32[]{:S(2)}) %collective-permute-start.3) | collective-permute-done | bytes 131104 | tf_op jit(solution)/shard_map/ppermute | solution.py:525
  21.5 1.3 %copy-done = f32[64,32,128]{2,1,0:T(8,128)S(1)} copy-done((f32[64,32,128]{2,1,0:T(8,128)S(1)}, f32[64,32,128]{2,1,0:T(8,128)}, u32[]{:S(2)}) %copy-start) | copy-done | bytes 1048600
  22.8 5.2 %rain.1 = f32[128,128]{1,0:T(8,128)} custom-call(s32[2]{0:T(128)S(1)} %copy-done.8, s32[128]{0:T(128)S(1)} %copy-done.9, s32[1]{0:T(128)} %get-tuple-element.15.bad_ref, f32[64,32,128]{2,1,0:T(8,128)S(1)} %copy-done, f32[128,128]{1,0:T(8,128)S(1)} %collective-permute-done.got_a_ref, f32[128,128]{1,0:T(8,128)S(1)} %collective-permute-done.1.got_b_ref, ...), custom_call_target="tpu_custom_call" | custom-call | flops 67108864 | bytes 2097152 | tf_op jit(solution)/shard_map/rain/pallas_call | solution.py:545
  28.0 10.3 %all-to-all-start = ((f32[128,1,128]{2,1,0:T(1,128)}), f32[128,1,128]{2,1,0:T(1,128)S(1)}, u32[]{:S(2)}, u32[]{:S(2)}) async-start(f32[128,1,128]{2,1,0:T(1,128)} %bitcast.7), calls=%async_computation | async-start | bytes 131072 | tf_op jit(solution)/shard_map/all_to_all | solution.py:556
  38.3 20.5 %mix.1 = f32[64,128,128]{2,1,0:T(8,128)} custom-call(s32[2]{0:T(128)} %pad_add_fusion.par_ref, s32[128]{0:T(128)} %cost_ref.3, s32[1]{0:T(128)} %get-tuple-element.15.bad_ref, f32[128,128]{1,0:T(8,128)} %mixing_ref.3, f32[128,128]{1,0:T(8,128)} %copy-done.12, f32[128,128]{1,0:T(8,128)} %copy-done.2, f32[128,128]{1,0:T(8,128)} %copy-done.3, ...), custom_call_target="tpu_custom_call" | custom-call | flops 4294967296 | bytes 10485760 | tf_op jit(solution)/shard_map/mix/pallas_call | solution.py:558
  58.8 1.1 %gather.1 = f32[16,128]{1,0:T(8,128)} custom-call(f32[128,128]{1,0:T(8,128)S(1)} %bitcast.11), custom_call_target="tpu_custom_call" | custom-call | flops 1048576 | bytes 1048576 | tf_op jit(solution)/shard_map/gather/pallas_call | solution.py:575
  (28 shorter events, 0.1 us)
Async XLA Ops:
  3.1 10.1 %copy-start.8 = (s32[2]{0:T(128)S(1)}, s32[2]{0:T(128)}, u32[]{:S(2)}) copy-start(s32[2]{0:T(128)} %pad_add_fusion.par_ref) | copy-start | bytes 28
  3.1 15.7 %copy-start.13 = (s32[64,32]{0,1:T(8,128)S(1)}, s32[64,32]{0,1:T(8,128)}, u32[]{:S(2)}) copy-start(s32[64,32]{0,1:T(8,128)} %param.11) | copy-start | bytes 24580
  3.1 16.0 %copy-start.10 = (f32[128,128]{1,0:T(8,128)S(1)}, f32[128,128]{1,0:T(8,128)}, u32[]{:S(2)}) copy-start(f32[128,128]{1,0:T(8,128)} %mixing_ref.3) | copy-start | bytes 196612
  3.1 16.0 %copy-start.11 = (s32[128]{0:T(128)S(1)}, s32[128]{0:T(128)}, u32[]{:S(2)}) copy-start(s32[128]{0:T(128)} %param.13) | copy-start | bytes 1540
  3.1 10.1 %collective-permute-start = (f32[128,128]{1,0:T(8,128)}, f32[128,128]{1,0:T(8,128)S(1)}, u32[]{:S(2)}, u32[]{:S(2)}) collective-permute-start(f32[128,128]{1,0:T(8,128)} %get-tuple-element.17), channel_id=1, source_target_pairs={{0,4},{4,0},{8,12},{12,8},{16,20},{20,16},{24,28},{28,24},{32,36},... | collective-permute-start | bytes 196616 | tf_op jit(solution)/shard_map/ppermute | solution.py:493
  4.6 16.9 %copy-start.9 = (s32[128]{0:T(128)S(1)}, s32[128]{0:T(128)}, u32[]{:S(2)}) copy-start(s32[128]{0:T(128)} %cost_ref.3) | copy-start | bytes 1540
  4.6 8.6 %collective-permute-start.1 = (f32[128,128]{1,0:T(8,128)}, f32[128,128]{1,0:T(8,128)S(1)}, u32[]{:S(2)}, u32[]{:S(2)}) collective-permute-start(f32[128,128]{1,0:T(8,128)} %get-tuple-element.18), channel_id=1, source_target_pairs={{0,124},{4,8},{8,4},{12,16},{16,12},{20,24},{24,20},{28,32},{32,28... | collective-permute-start | bytes 196616 | tf_op jit(solution)/shard_map/ppermute | solution.py:494
  13.2 25.1 %copy-start.2 = (f32[128,128]{1,0:T(8,128)}, f32[128,128]{1,0:T(8,128)S(1)}, u32[]{:S(2)}) copy-start(f32[128,128]{1,0:T(8,128)S(1)} %collective-permute-done.got_a_ref) | copy-start | bytes 196612
  13.2 25.1 %copy-start.3 = (f32[128,128]{1,0:T(8,128)}, f32[128,128]{1,0:T(8,128)S(1)}, u32[]{:S(2)}) copy-start(f32[128,128]{1,0:T(8,128)S(1)} %collective-permute-done.1.got_b_ref) | copy-start | bytes 196612
  13.2 1.0 %copy-start.1 = (f32[64,8,128]{2,1,0:T(8,128)S(1)}, f32[64,8,128]{2,1,0:T(8,128)}, u32[]{:S(2)}) copy-start(f32[64,8,128]{2,1,0:T(8,128)} %get-tuple-element.19.edge_ref) | copy-start | bytes 786436
  14.8 6.1 %collective-permute-start.2 = (f32[64,4,128]{2,1,0:T(4,128)S(1)}, f32[64,4,128]{2,1,0:T(4,128)S(1)}, u32[]{:S(2)}, u32[]{:S(2)}) collective-permute-start(f32[64,4,128]{2,1,0:T(4,128)S(1)} %get-tuple-element.20), channel_id=1, source_target_pairs={{0,1},{1,0},{2,3},{3,2},{4,5},{5,4},{6,7},{7,6},{8,9},{9,8},{10,11... | collective-permute-start | bytes 393224 | tf_op jit(solution)/shard_map/ppermute | solution.py:524
  16.5 5.0 %collective-permute-start.3 = (f32[64,4,128]{2,1,0:T(4,128)S(1)}, f32[64,4,128]{2,1,0:T(4,128)S(1)}, u32[]{:S(2)}, u32[]{:S(2)}) collective-permute-start(f32[64,4,128]{2,1,0:T(4,128)S(1)} %get-tuple-element.21), channel_id=1, source_target_pairs={{0,3},{1,2},{2,1},{3,0},{4,7},{5,6},{6,5},{7,4},{8,11},{9,10},{10,... | collective-permute-start | bytes 393224 | tf_op jit(solution)/shard_map/ppermute | solution.py:525
  20.8 7.2 %copy-start.12 = (f32[128,128]{1,0:T(8,128)}, f32[128,128]{1,0:T(8,128)S(1)}, u32[]{:S(2)}) copy-start(f32[128,128]{1,0:T(8,128)S(1)} %get-tuple-element.16.mask_ref) | copy-start | bytes 196612
  20.8 17.5 %copy-start.6 = (bf16[256,256]{1,0:T(8,128)(2,1)}, bf16[256,256]{1,0:T(8,128)(2,1)S(1)}, u32[]{:S(2)}) copy-start(bf16[256,256]{1,0:T(8,128)(2,1)S(1)} %get-tuple-element.22.first_ref) | copy-start | bytes 393220
  20.8 17.5 %copy-start.7 = (bf16[256,128]{1,0:T(8,128)(2,1)}, bf16[256,128]{1,0:T(8,128)(2,1)S(1)}, u32[]{:S(2)}) copy-start(bf16[256,128]{1,0:T(8,128)(2,1)S(1)} %get-tuple-element.23.second_ref) | copy-start | bytes 196612
  20.8 17.5 %copy-start.4 = (f32[64,4,128]{2,1,0:T(4,128)}, f32[64,4,128]{2,1,0:T(4,128)S(1)}, u32[]{:S(2)}) copy-start(f32[64,4,128]{2,1,0:T(4,128)S(1)} %collective-permute-done.2.got_c_ref) | copy-start | bytes 393220
  21.5 16.8 %copy-start.5 = (f32[64,4,128]{2,1,0:T(4,128)}, f32[64,4,128]{2,1,0:T(4,128)S(1)}, u32[]{:S(2)}) copy-start(f32[64,4,128]{2,1,0:T(4,128)S(1)} %collective-permute-done.3.got_d_ref) | copy-start | bytes 393220
  21.5 1.3 %copy-start = (f32[64,32,128]{2,1,0:T(8,128)S(1)}, f32[64,32,128]{2,1,0:T(8,128)}, u32[]{:S(2)}) copy-start(f32[64,32,128]{2,1,0:T(8,128)} %get-tuple-element.25.tracer_ref) | copy-start | bytes 3145732
  28.0 30.9 %all-to-all-start = ((f32[128,1,128]{2,1,0:T(1,128)}), f32[128,1,128]{2,1,0:T(1,128)S(1)}, u32[]{:S(2)}, u32[]{:S(2)}) async-start(f32[128,1,128]{2,1,0:T(1,128)} %bitcast.7), calls=%async_computation | async-start | bytes 131072 | tf_op jit(solution)/shard_map/all_to_all | solution.py:556
where the time goes:
time: 60.2 us; the launch traced here: 59.9 us
  Pallas kernels  38.1 us (63%)
  starting transfers between devices  17 us (28%)
  local copies, waits for them, and re-layouts  2.63 us (4%)
  between operations  0.88 us (1%)
  waiting for transfers between devices  0.68 us (1%)
  other arithmetic  0.61 us (1%)
    pallas_call x1, Pallas kernels, body(): pl.pallas_call(mix_kernel, out_shape=struct(px, rows, lev), in_specs=[SME...  20.5 us
    all_to_all x1, starting transfers between devices, body(): lax.all_to_all(outgoing, ('elem', 'blk'), split_axis=0, concat_axis=0, ti...  10.3 us
    pallas_call x1, Pallas kernels, body(): pl.pallas_call(local_kernel, out_shape=(struct(px, rows, lev), struct(px,...  7.26 us
    pallas_call x1, Pallas kernels, body(): pl.pallas_call(rain_kernel, out_shape=struct(groups, lev), in_specs=[SMEM...  5.18 us
    unnamed x29, local copies, waits for them, and re-layouts  2.37 us
    ppermute x1, starting transfers between devices, body(): got_d = lax.ppermute(send_d, 'blk', pair_d)  2.24 us
    pallas_call x1, Pallas kernels, body(): pl.pallas_call(sides_kernel, grid=(1,), out_shape=(struct(rows, lev),) *...  1.81 us
    ppermute x1, starting transfers between devices, body(): got_c = lax.ppermute(send_c, 'blk', pair_c)  1.72 us
  transfers between devices with their start and end apart: 5, of which 1 were waited for; matrix products, arithmetic and copies ran while one was open for 1% of the time, Pallas kernels for 49%

commit v1 on v0

--- a/solution.py
+++ b/solution.py
@@ -72,7 +72,7 @@
     return lax.broadcasted_iota(jnp.int32, shape, dim)
 
 
-def gains_kernel(mixing_ref, dest_ref, trig_ref, gain_ref, onehot_ref, mask_ref, first_ref, second_ref, bad_ref, sums):
+def gains_kernel(mixing_ref, dest_ref, trig_ref, gain_ref, onehot_ref, lanes_ref, first_ref, second_ref, bad_ref, sums):
     square = mixing_ref[...]
     worst = jnp.max(jnp.abs(square))
     first_ref[...], second_ref[...] = weights(*split3(square.T))
@@ -108,10 +108,15 @@
     onehot_ref[1] = jnp.where(at & (within == 1), 1.0, 0.0).astype(BF16)
 
     px, py = trig_ref.shape
-    rows = py * NT
-    trig = jnp.concatenate([trig_ref[...].astype(F32), jnp.zeros((LEV - px, py), F32)], axis=0).T
-    spread = jnp.where(iota((rows, py), 0) // NT == iota((rows, py), 1), 1.0, 0.0).astype(BF16)
-    mask_ref[...] = mm(spread, trig.astype(BF16))
+    half = py // 2
+    wide = trig_ref[...].astype(F32).astype(BF16)
+    table = jnp.zeros((groups, LEV), F32)
+    for h in range(2):
+        chosen = jnp.where(iota((groups, px), 0) == 2 * iota((groups, px), 1) + h, 1.0, 0.0).astype(BF16)
+        lane = iota((py, LEV), 1)
+        placed = jnp.where((lane < 2 * half) & (lane % half + half * h == iota((py, LEV), 0)), 1.0, 0.0).astype(BF16)
+        table = table + mm(mm(chosen, wide).astype(BF16), placed)
+    lanes_ref[...] = table
 
 
 def half_coefs(first, second):
@@ -141,20 +146,29 @@
             store(a, 16 * k + 8 * h, wx * along_x + wy * along_y)
 
 
-def sides_kernel(par_ref, low_ref, high_ref, low_x_ref, high_x_ref, low_y_ref, high_y_ref, send_a_ref, send_b_ref, first_ref, final_ref):
-    even = par_ref[0] == 0
-    for k in range(low_ref.shape[1] // 16):
-        for ref, x_ref, y_ref, out_ref, at in ((low_ref, low_x_ref, low_y_ref, first_ref, 0), (high_ref, high_x_ref, high_y_ref, final_ref, NP - 1)):
-            def load(a, i, ref=ref):
-                return ref[a, i:i + 8, :]
-
-            def store(a, i, value, out_ref=out_ref):
-                out_ref[i:i + 8, :] = value
-
-            tendency(k, (at,), load, lambda a, y, ref=x_ref: ref[0, y:y + 1, :], lambda a, y, ref=y_ref: ref[0, y:y + 1, :], store)
-    first, final = first_ref[...], final_ref[...]
-    send_a_ref[...] = jnp.where(even, final, first)
-    send_b_ref[...] = jnp.where(even, first, final)
+def sides_kernel(state_hbm, wx_hbm, wy_hbm, send_a_ref, send_b_ref, state, wx, wy, ends, sems):
+    even = lax.axis_index("elem") % 2 == 0
+    px = state_hbm.shape[0]
+    copies = []
+    for i, (element, x) in enumerate(((0, 0), (px - NP, px - 1))):
+        copies.append(pltpu.make_async_copy(state_hbm.at[pl.ds(element, NP)], state.at[i], sems.at[i]))
+        copies.append(pltpu.make_async_copy(wx_hbm.at[x], wx.at[i], sems.at[2 + i]))
+        copies.append(pltpu.make_async_copy(wy_hbm.at[x], wy.at[i], sems.at[4 + i]))
+    for copy in copies:
+        copy.start()
+    for copy in copies:
+        copy.wait()
+    for k in range(state.shape[2] // 16):
+        for s, at in ((0, 0), (1, NP - 1)):
+            def load(a, i):
+                return state[s, a, i:i + 8, :]
+
+            def store(a, i, value):
+                ends[s, i:i + 8, :] = value
+
+            tendency(k, (at,), load, lambda a, y: wx[s, y:y + 1, :], lambda a, y: wy[s, y:y + 1, :], store)
+    send_a_ref[...] = jnp.where(even, ends[1], ends[0])
+    send_b_ref[...] = jnp.where(even, ends[0], ends[1])
 
 
 def smooth_rows(v, up, down):
@@ -172,28 +186,16 @@
     return out
 
 
-def local_kernel(state_hbm, wx_hbm, wy_hbm, adv_hbm, tracer_ref, edge_ref, state, wx, wy, tend, adv, sems, out_sems):
+def local_kernel(state, wx, wy, adv_hbm, tracer_ref, edge_ref, tend, adv, sems):
     elements = state.shape[0] // NP
     rows = state.shape[1]
     lower = iota((8, LEV), 0) < 4
 
-    def piece(e):
-        return pl.ds(e * NP, NP)
-
-    def copies(e):
-        return [pltpu.make_async_copy(src.at[piece(e)], dst.at[piece(e)], sems.at[i, e]) for i, (src, dst) in enumerate(((state_hbm, state), (wx_hbm, wx), (wy_hbm, wy)))]
-
     def out_copy(e):
-        return pltpu.make_async_copy(adv.at[piece(e)], adv_hbm.at[piece(e)], out_sems.at[e])
-
-    for e in range(elements):
-        for copy in copies(e):
-            copy.start()
+        piece = pl.ds(e * NP, NP)
+        return pltpu.make_async_copy(adv.at[piece], adv_hbm.at[piece], sems.at[e])
 
     def differentiate(e):
-        for copy in copies(e):
-            copy.wait()
-
         def load(a, i):
             return state[e * NP + a, i:i + 8, :]
 
@@ -234,9 +236,9 @@
         out_copy(e).wait()
 
 
-def edge_kernel(par_ref, edge_ref, got_a_ref, got_b_ref, send_c_ref, send_d_ref):
-    even = par_ref[0] == 0
-    even_y = par_ref[1] == 0
+def edge_kernel(edge_ref, got_a_ref, got_b_ref, send_c_ref, send_d_ref):
+    even = lax.axis_index("elem") % 2 == 0
+    even_y = lax.axis_index("blk") % 2 == 0
     px = edge_ref.shape[0]
     rows = got_a_ref.shape[0]
     lower = iota((8, LEV), 0) < 4
@@ -258,12 +260,12 @@
     return smooth_rows(before, None, None), smooth_rows(after, None, None)
 
 
-def rain_kernel(par_ref, cost_ref, bad_ref, tracer_ref, got_a_ref, got_b_ref, got_c_ref, got_d_ref, mask_ref, gain_ref, onehot_ref, first_ref, second_ref, out_ref, rain_ref, side_ref, z_ref):
+def rain_kernel(cost_ref, bad_ref, tracer_ref, got_a_ref, got_b_ref, got_c_ref, got_d_ref, mask_ref, gain_ref, onehot_ref, first_ref, second_ref, out_ref, rain_ref, side_ref):
     px, py, _ = tracer_ref.shape
     half = py // 2
     rows = py * NT
-    even_y = par_ref[1] == 0
-    for s, side in enumerate(side_shares(par_ref[0] == 0, got_a_ref, got_b_ref, rows)):
+    even_y = lax.axis_index("blk") % 2 == 0
+    for s, side in enumerate(side_shares(lax.axis_index("elem") % 2 == 0, got_a_ref, got_b_ref, rows)):
         for i, value in enumerate(side):
             side_ref[s, 8 * i:8 * i + 8, :] = value
     at_first = iota((half, LEV), 0) == 0
@@ -279,7 +281,6 @@
             return low + extra[0:half], high + extra[half:py]
         return low, high
 
-    ones = jnp.ones((2 * LEV, LEV), BF16)
     place = (iota((half, LEV), 1) < 2 * half) & (iota((half, LEV), 1) % half == iota((half, LEV), 0))
 
     def weigh(x, part, h):
@@ -288,10 +289,11 @@
     def step_by_step(x, part, h):
         return part - repeated(part, cost_ref[2 * x + h], first_ref, second_ref)
 
-    def fill(rule):
+    def fill(rule, unroll):
         def one(x):
             for h, part in enumerate(advanced(x)):
-                z_ref[x, half * h:half * h + half, :] = rule(x, part, h)
+                sums = jnp.sum(rule(x, part, h), axis=1, keepdims=True) * 0.125
+                rain_ref[pl.ds(2 * x + h, 1), :] = jnp.sum(jnp.where(place, sums, 0.0), axis=0, keepdims=True)
 
         one(0)
         one(px - 1)
@@ -300,110 +302,156 @@
             one(x)
             return carry
 
-        lax.fori_loop(1, px - 1, step, 0, unroll=2)
+        lax.fori_loop(1, px - 1, step, 0, unroll=unroll)
 
     @pl.when(bad_ref[0] == 0)
     def _():
-        fill(weigh)
+        fill(weigh, 31)
 
     @pl.when(bad_ref[0] != 0)
     def _():
-        fill(step_by_step)
-
-    def total(x, carry):
-        high, low = split2(z_ref[x])
-        sums = mm(jnp.concatenate([high, low], axis=1), ones) * 0.125
-        for h in range(2):
-            spread = jnp.where(place, sums[half * h:half * h + half], 0.0)
-            rain_ref[pl.ds(2 * x + h, 1), :] = jnp.sum(spread, axis=0, keepdims=True)
-        return carry
-
-    lax.fori_loop(0, px, total, 0, unroll=4)
+        fill(step_by_step, 1)
+
     lane = iota(out_ref.shape, 1)
-    values = jnp.where(lane == 2 * half, 1.0, jnp.where(mask_ref[...] > 0, rain_ref[...], 0.0))
+    values = jnp.where(lane == 2 * half, 1.0, jnp.where(mask_ref[...] > 0.5, rain_ref[...], 0.0))
     first = exact_pick(onehot_ref[0], values)
     second = exact_pick(onehot_ref[1], values)
     out_ref[...] = jnp.where(lane < half, first, jnp.where(lane < 2 * half, second, first + second))
 
 
-def mix_kernel(par_ref, cost_ref, bad_ref, mixing_ref, mask_ref, got_a_ref, got_b_ref, got_c_ref, got_d_ref, first_ref, second_ref, adv_hbm, new_hbm, adv, new, powers, sems, out_sems):
+def mix_kernel(cost_ref, bad_ref, mixing_hbm, trig_hbm, got_a_hbm, got_b_hbm, got_c_hbm, got_d_hbm, first_hbm, second_hbm, adv_hbm, new_hbm, adv, new, powers, mixing_ref, trig_ref, got_a_ref, got_b_ref, got_c_ref, got_d_ref, first_ref, second_ref, mask_ref, sems, out_sems, small_sems):
     px, rows, _ = adv.shape
+    py = rows // NT
     half = rows // 2
-    elements = px // NP
-    even_y = par_ref[1] == 0
+    chunks = sems.shape[0]
+    size = px // chunks
+    even_y = lax.axis_index("blk") % 2 == 0
     lower = iota((8, LEV), 0) < 4
 
-    def piece(e):
-        return pl.ds(e * NP, NP)
-
-    def in_copy(e):
-        return pltpu.make_async_copy(adv_hbm.at[piece(e)], adv.at[piece(e)], sems.at[e])
-
-    def out_copy(e):
-        return pltpu.make_async_copy(new.at[piece(e)], new_hbm.at[piece(e)], out_sems.at[e])
-
-    for e in range(elements):
-        in_copy(e).start()
+    def in_copy(i):
+        return pltpu.make_async_copy(adv_hbm.at[pl.ds(i * size, size)], adv.at[pl.ds(i * size, size)], sems.at[i])
+
+    def out_copy(i):
+        return pltpu.make_async_copy(new.at[pl.ds(i * size, size)], new_hbm.at[pl.ds(i * size, size)], out_sems.at[i])
+
+    small = [
+        pltpu.make_async_copy(src, dst, small_sems.at[i])
+        for i, (src, dst) in enumerate(
+            (
+                (mixing_hbm, mixing_ref),
+                (trig_hbm, trig_ref),
+                (got_a_hbm, got_a_ref),
+                (got_b_hbm, got_b_ref),
+                (got_c_hbm, got_c_ref),
+                (got_d_hbm, got_d_ref),
+                (first_hbm, first_ref),
+                (second_hbm, second_ref),
+            )
+        )
+    ]
+    for copy in small:
+        copy.start()
+    for i in range(chunks):
+        in_copy(i).start()
+    small[0].wait()
 
     @pl.when(bad_ref[0] == 0)
     def _():
         powers[0] = jnp.concatenate(split3(mixing_ref[...].T), axis=1)
-        for k in (1, 2, 4, 8, 16, 32):
-            def part(j):
-                return powers[j, :, 0:LEV], powers[j, :, LEV:2 * LEV], powers[j, :, 2 * LEV:3 * LEV]
-
+
+        def part(j):
+            return powers[j, :, 0:LEV], powers[j, :, LEV:2 * LEV], powers[j, :, 2 * LEV:3 * LEV]
+
+        for k in (1, 2, 4, 8):
             first, second = weights(*part(k - 1))
 
             def step(j, carry):
                 powers[j + k] = jnp.concatenate(split3(precise(*part(j), first, second)), axis=1)
                 return carry
 
-            lax.fori_loop(0, k, step, 0, unroll=min(k, 4))
-
-    shares = side_shares(par_ref[0] == 0, got_a_ref, got_b_ref, rows)
-    for e, x, share in ((0, 0, shares[0]), (elements - 1, px - 1, shares[1])):
-        in_copy(e).wait()
+            lax.fori_loop(0, k, step, 0, unroll=True)
+
+        for k in (16, 32):
+            pair = powers[k - 1, :, 0:2 * LEV]
+            both = jnp.concatenate([pair, pair], axis=0)
+
+            def later(j, carry):
+                value = mm(powers[j, :, 0:2 * LEV], both)
+                powers[j + k, :, 0:2 * LEV] = jnp.concatenate(split2(value[:, :LEV] + value[:, LEV:]), axis=1)
+                return carry
+
+            lax.fori_loop(0, k, later, 0, unroll=8)
+
+    for copy in small[1:]:
+        copy.wait()
+    trig = jnp.concatenate([trig_ref[...].astype(F32), jnp.zeros((LEV - px, py), F32)], axis=0).T
+    spread = jnp.where(iota((rows, py), 0) // NT == iota((rows, py), 1), 1.0, 0.0).astype(BF16)
+    mask_ref[...] = mm(spread, trig.astype(BF16))
+    shares = side_shares(lax.axis_index("elem") % 2 == 0, got_a_ref, got_b_ref, rows)
+    in_copy(0).wait()
+    in_copy(chunks - 1).wait()
+    for x, share in ((0, shares[0]), (px - 1, shares[1])):
         for i in range(rows // 8):
             adv[x, 8 * i:8 * i + 8, :] = adv[x, 8 * i:8 * i + 8, :] + share[i]
 
-    def element(e, carry):
-        @pl.when((e > 0) & (e < elements - 1))
+    def edged(x, h):
+        start = adv[x, half * h:half * h + half, :]
+        if h == 0:
+            add = 0.5 * jnp.where(even_y, got_d_ref[x], got_c_ref[x])
+            return jnp.concatenate([start[0:8] + jnp.where(lower, jnp.concatenate([add, add], axis=0), 0.0), start[8:]], axis=0)
+        add = 0.5 * jnp.where(even_y, got_c_ref[x], got_d_ref[x])
+        return jnp.concatenate([start[:half - 8], start[half - 8:] + jnp.where(lower, 0.0, jnp.concatenate([add, add], axis=0))], axis=0)
+
+    def powered(x, h, start):
+        high, low = split2(start)
+        both = mm(jnp.concatenate([high, low], axis=0), powers[cost_ref[2 * x + h] - 1, :, 0:2 * LEV])
+        return (both[:half, :LEV] + both[half:, :LEV]) + (both[:half, LEV:] + both[half:, LEV:])
+
+    def step_by_step(x, h, start):
+        return repeated(start, cost_ref[2 * x + h], first_ref, second_ref)
+
+    def one(rule, x, mask):
+        for h in range(2):
+            start = edged(x, h)
+            done = rule(x, h, start)
+            new[x, half * h:half * h + half, :] = jnp.where(mask[half * h:half * h + half] > 0.5, done, start)
+
+    def arrive(i):
+        @pl.when((i > 0) & (i < chunks - 1))
         def _():
-            in_copy(e).wait()
-
-        rolled = pltpu.roll(mask_ref[...], lax.rem(LEV - e * NP, LEV), axis=1)
-        for a in range(NP):
-            x = e * NP + a
-            up = 0.5 * jnp.where(even_y, got_d_ref[x], got_c_ref[x])
-            down = 0.5 * jnp.where(even_y, got_c_ref[x], got_d_ref[x])
-            adv[x, 0:4, :] = adv[x, 0:4, :] + up
-            adv[x, rows - 4:rows, :] = adv[x, rows - 4:rows, :] + down
-            mask = jnp.broadcast_to(rolled[:, a:a + 1], (rows, LEV))
-
-            @pl.when(bad_ref[0] == 0)
-            def _():
-                for h in range(2):
-                    part = slice(half * h, half * h + half)
-                    start = adv[x, part, :]
-                    high, low = split2(start)
-                    both = mm(jnp.concatenate([high, low], axis=0), powers[cost_ref[2 * x + h] - 1, :, 0:2 * LEV])
-                    done = (both[:half, :LEV] + both[half:, :LEV]) + (both[:half, LEV:] + both[half:, LEV:])
-                    new[x, part, :] = jnp.where(mask[part] > 0.5, done, start)
-
-            @pl.when(bad_ref[0] != 0)
-            def _():
-                for h in range(2):
-                    part = slice(half * h, half * h + half)
-                    start = adv[x, part, :]
-                    done = repeated(start, cost_ref[2 * x + h], first_ref, second_ref)
-                    new[x, part, :] = jnp.where(mask[part] > 0.5, done, start)
-
-        out_copy(e).start()
-        return carry
-
-    lax.fori_loop(0, elements, element, 0)
-    for e in range(elements):
-        out_copy(e).wait()
+            in_copy(i).wait()
+
+    @pl.when(bad_ref[0] == 0)
+    def _():
+        def chunk(i, carry):
+            arrive(i)
+            rolled = pltpu.roll(mask_ref[...], lax.rem(LEV - i * size, LEV), axis=1)
+            for a in range(size):
+                one(powered, i * size + a, jnp.broadcast_to(rolled[:, a:a + 1], (rows, LEV)))
+            out_copy(i).start()
+            return carry
+
+        lax.fori_loop(0, chunks, chunk, 0)
+
+    @pl.when(bad_ref[0] != 0)
+    def _():
+        def chunk(i, carry):
+            arrive(i)
+
+            def column(a, carry):
+                x = i * size + a
+                rolled = pltpu.roll(mask_ref[...], lax.rem(LEV - x, LEV), axis=1)
+                one(step_by_step, x, jnp.broadcast_to(rolled[:, 0:1], (rows, LEV)))
+                return carry
+
+            lax.fori_loop(0, size, column, 0)
+            out_copy(i).start()
+            return carry
+
+        lax.fori_loop(0, chunks, chunk, 0)
+
+    for i in range(chunks):
+        out_copy(i).wait()
 
 
 def gather_kernel(got_ref, rain_ref):
@@ -457,34 +505,31 @@
     elements = px // NP
     n_elem, n_blk = lax.axis_size("elem"), lax.axis_size("blk")
     slabs = state.reshape(px, rows, lev)
-    parity = jnp.stack([lax.axis_index("elem") % 2, lax.axis_index("blk") % 2]).astype(jnp.int32)
-    lanes = jnp.pad(jnp.tile(triggers.reshape(groups, GROUP_COLS), (1, 2)), ((0, 0), (0, lev - 2 * GROUP_COLS)))
-
     def struct(*shape, dtype=F32):
         return jax.ShapeDtypeStruct(shape, dtype)
 
     def block(shape, *at):
         return pl.BlockSpec(shape, lambda i: at)
 
+    def kept(x):
+        return pltpu.with_memory_space_constraint(x, pltpu.HBM)
+
     send_a, send_b = pl.pallas_call(
         sides_kernel,
-        grid=(1,),
         out_shape=(struct(rows, lev),) * 2,
-        in_specs=[
-            SMEM,
-            block((NP, rows, lev), 0, 0, 0),
-            block((NP, rows, lev), elements - 1, 0, 0),
-            block((1, py, lev), 0, 0, 0),
-            block((1, py, lev), px - 1, 0, 0),
-            block((1, py, lev), 0, 0, 0),
-            block((1, py, lev), px - 1, 0, 0),
+        in_specs=[HBM] * 3,
+        out_specs=(VMEM, VMEM),
+        scratch_shapes=[
+            pltpu.VMEM((2, NP, rows, lev), F32),
+            pltpu.VMEM((2, py, lev), F32),
+            pltpu.VMEM((2, py, lev), F32),
+            pltpu.VMEM((2, rows, lev), F32),
+            pltpu.SemaphoreType.DMA((6,)),
         ],
-        out_specs=(block((rows, lev), 0, 0),) * 2,
-        scratch_shapes=[pltpu.VMEM((rows, lev), F32)] * 2,
-        compiler_params=params(60),
+        compiler_params=params(4),
         cost_estimate=cost(2 * MIB, MIB),
         name="sides",
-    )(parity, slabs, slabs, wind_x, wind_x, wind_y, wind_y)
+    )(kept(slabs), kept(wind_x), kept(wind_y))
 
     pair_a = [(i, i ^ 1) for i in range(n_elem)]
     pair_b = [(i, (i - 1 if i % 2 == 0 else i + 1) % n_elem) for i in range(n_elem)]
@@ -495,19 +540,15 @@
 
     local, tracer, edges = pl.pallas_call(
         local_kernel,
-        out_shape=(struct(px, rows, lev), struct(px, py, lev), struct(px, 8, lev)),
-        in_specs=[HBM, HBM, HBM],
+        out_shape=(pltpu.HBM((px, rows, lev), F32), struct(px, py, lev), struct(px, 8, lev)),
+        in_specs=[VMEM, VMEM, VMEM],
         out_specs=(HBM, VMEM, VMEM),
         scratch_shapes=[
             pltpu.VMEM((px, rows, lev), F32),
-            pltpu.VMEM((px, py, lev), F32),
-            pltpu.VMEM((px, py, lev), F32),
             pltpu.VMEM((px, rows, lev), F32),
-            pltpu.VMEM((px, rows, lev), F32),
-            pltpu.SemaphoreType.DMA((3, elements)),
             pltpu.SemaphoreType.DMA((elements,)),
         ],
-        compiler_params=params(60),
+        compiler_params=params(14),
         cost_estimate=cost(64 * MIB, 12 * MIB),
         name="local",
     )(slabs, wind_x, wind_y)
@@ -515,21 +556,21 @@
     send_c, send_d = pl.pallas_call(
         edge_kernel,
         out_shape=(struct(px, nt, lev),) * 2,
-        in_specs=[SMEM, VMEM, VMEM, VMEM],
+        in_specs=[VMEM, VMEM, VMEM],
         out_specs=(VMEM, VMEM),
         compiler_params=params(8),
         cost_estimate=cost(MIB, MIB),
         name="edges",
-    )(parity, edges, got_a, got_b)
+    )(edges, got_a, got_b)
     got_c = lax.ppermute(send_c, "blk", pair_c)
     got_d = lax.ppermute(send_d, "blk", pair_d)
 
-    gains, onehots, mask, first, second, bad = pl.pallas_call(
+    gains, onehots, lanes, first, second, bad = pl.pallas_call(
         gains_kernel,
         out_shape=(
             struct(MAXC, lev),
             struct(2, groups, groups, dtype=BF16),
-            struct(rows, lev),
+            struct(groups, lev),
             struct(2 * lev, 2 * lev, dtype=BF16),
             struct(2 * lev, lev, dtype=BF16),
             struct(1, dtype=jnp.int32),
@@ -545,32 +586,43 @@
     outgoing = pl.pallas_call(
         rain_kernel,
         out_shape=struct(groups, lev),
-        in_specs=[SMEM, SMEM, SMEM] + [VMEM] * 10,
+        in_specs=[SMEM, SMEM] + [VMEM] * 10,
         out_specs=VMEM,
-        scratch_shapes=[pltpu.VMEM((groups, lev), F32), pltpu.VMEM((2, rows, lev), F32), pltpu.VMEM((px, py, lev), F32)],
+        scratch_shapes=[pltpu.VMEM((groups, lev), F32), pltpu.VMEM((2, rows, lev), F32)],
         compiler_params=params(12),
         cost_estimate=cost(64 * MIB, 2 * MIB),
         name="rain",
-    )(parity, group_costs, bad, tracer, got_a, got_b, got_c, got_d, lanes, gains, onehots, first, second)
+    )(group_costs, bad, tracer, got_a, got_b, got_c, got_d, lanes, gains, onehots, first, second)
 
     incoming = lax.all_to_all(outgoing, ("elem", "blk"), split_axis=0, concat_axis=0, tiled=True)
 
+    chunks = 4
     new = pl.pallas_call(
         mix_kernel,
         out_shape=struct(px, rows, lev),
-        in_specs=[SMEM, SMEM, SMEM] + [VMEM] * 8 + [HBM],
+        in_specs=[SMEM, SMEM] + [HBM] * 9,
         out_specs=HBM,
         scratch_shapes=[
             pltpu.VMEM((px, rows, lev), F32),
             pltpu.VMEM((px, rows, lev), F32),
             pltpu.VMEM((MAXC, lev, 3 * lev), BF16),
-            pltpu.SemaphoreType.DMA((elements,)),
-            pltpu.SemaphoreType.DMA((elements,)),
+            pltpu.VMEM((lev, lev), F32),
+            pltpu.VMEM((px, py), jnp.int32),
+            pltpu.VMEM((rows, lev), F32),
+            pltpu.VMEM((rows, lev), F32),
+            pltpu.VMEM((px, nt, lev), F32),
+            pltpu.VMEM((px, nt, lev), F32),
+            pltpu.VMEM((2 * lev, 2 * lev), BF16),
+            pltpu.VMEM((2 * lev, lev), BF16),
+            pltpu.VMEM((rows, lev), F32),
+            pltpu.SemaphoreType.DMA((chunks,)),
+            pltpu.SemaphoreType.DMA((chunks,)),
+            pltpu.SemaphoreType.DMA((8,)),
         ],
         compiler_params=params(60),
         cost_estimate=cost(4096 * MIB, 10 * MIB),
         name="mix",
-    )(parity, group_costs, bad, mixing, mask, got_a, got_b, got_c, got_d, first, second, local)
+    )(group_costs, bad, mixing, triggers, got_a, got_b, got_c, got_d, first, second, kept(local))
 
     rain = pl.pallas_call(
         gather_kernel,

time: 60.2 us -> 41.1 us (0.68)
  Pallas kernels: 38.1 us -> 21.1 us
  local copies, waits for them, and re-layouts: 2.63 us -> 0.14 us
  starting transfers between devices: 17 us -> 17.9 us
  other arithmetic: 0.61 us -> 0 us
    pallas_call x1, Pallas kernels: 20.5 us -> 9.47 us  [body(): pl.pallas_call(mix_kernel, out_shape=struct(px, rows, lev), in_specs=[SME...]
    pallas_call x2, Pallas kernels: 9.07 us -> 6.13 us  [the longest x1 4.77 us: body(): pl.pallas_call(local_kernel, out_shape=(pltpu.HBM((px, rows, lev), F32),...]
    pallas_call x1, Pallas kernels: 5.18 us -> 2.6 us  [body(): pl.pallas_call(rain_kernel, out_shape=struct(groups, lev), in_specs=[SMEM...]
    unnamed x29, local copies, waits for them, and re-layouts: 2.37 us -> 0.14 us
    all_to_all x1, starting transfers between devices: 10.3 us -> 11.1 us  [body(): lax.all_to_all(outgoing, ('elem', 'blk'), split_axis=0, concat_axis=0, ti...]
    another operation x1 -> x0, other arithmetic: 0.61 us -> none  [body(): jnp.stack([lax.axis_index('elem') % 2, lax.axis_index('blk') % 2])]
  transfers between devices with their start and end apart: 5 -> 5, of which waited for: 1 -> 2; matrix products, arithmetic and copies ran while one was open for 1% -> 0% of each run, Pallas kernels for 49% -> 39%
where the time goes in v1:
time: 41.1 us; the launch traced here: 41 us
  Pallas kernels  21.1 us (51%)
  starting transfers between devices  17.9 us (44%)
  waiting for transfers between devices  0.98 us (2%)
  between operations  0.87 us (2%)
    all_to_all x1, starting transfers between devices, body(): lax.all_to_all(outgoing, ('elem', 'blk'), split_axis=0, concat_axis=0, ti...  11.1 us
    pallas_call x1, Pallas kernels, body(): pl.pallas_call(mix_kernel, out_shape=struct(px, rows, lev), in_specs=[SME...  9.47 us
    pallas_call x1, Pallas kernels, body(): pl.pallas_call(local_kernel, out_shape=(pltpu.HBM((px, rows, lev), F32),...  4.77 us
    pallas_call x1, Pallas kernels, body(): pl.pallas_call(rain_kernel, out_shape=struct(groups, lev), in_specs=[SMEM...  2.6 us
    ppermute x1, starting transfers between devices, body(): got_d = lax.ppermute(send_d, 'blk', pair_d)  2.24 us
    pallas_call x1, Pallas kernels, body(): pl.pallas_call(gains_kernel, out_shape=(struct(MAXC, lev), struct(2, grou...  1.75 us
    ppermute x1, starting transfers between devices, body(): got_c = lax.ppermute(send_c, 'blk', pair_c)  1.72 us
    ppermute x1, starting transfers between devices, body(): got_a = lax.ppermute(send_a, 'elem', pair_a)  1.5 us
  transfers between devices with their start and end apart: 5, of which 2 were waited for; matrix products, arithmetic and copies ran while one was open for 0% of the time, Pallas kernels for 39%

profile of v1, /device:TPU:1, one launch (start us, length us, event | category | flops | bytes accessed | tf_op | source)
XLA Modules:
  0.0 41.0 jit_solution(4375738249122091536)
XLA Ops:
  0.7 1.4 %sides.1 = (f32[128,128]{1,0:T(8,128)S(1)}, f32[128,128]{1,0:T(8,128)S(1)}) custom-call(f32[64,128,128]{2,1,0:T(8,128)} %bitcast.8, f32[64,32,128]{2,1,0:T(8,128)} %wx.1, f32[64,32,128]{2,1,0:T(8,128)} %wy.1), custom_call_target="tpu_custom_call" | custom-call | flops 2097152 | bytes 1048576 | tf_op jit(solution)/shard_map/sides/pallas_call | solution.py:517
  2.0 0.0 copy-start.13
  2.0 0.0 copy-start.11
  2.1 0.0 copy-start.12
  2.1 1.5 %collective-permute-start = (f32[128,128]{1,0:T(8,128)S(1)}, f32[128,128]{1,0:T(8,128)S(1)}, u32[]{:S(2)}, u32[]{:S(2)}) collective-permute-start(f32[128,128]{1,0:T(8,128)S(1)} %get-tuple-element.16), channel_id=1, source_target_pairs={{0,4},{4,0},{8,12},{12,8},{16,20},{20,16},{24,28},{28,24},{32,36},... | collective-permute-start | bytes 196616 | tf_op jit(solution)/shard_map/ppermute | solution.py:538
  3.6 1.3 %collective-permute-start.1 = (f32[128,128]{1,0:T(8,128)S(1)}, f32[128,128]{1,0:T(8,128)S(1)}, u32[]{:S(2)}, u32[]{:S(2)}) collective-permute-start(f32[128,128]{1,0:T(8,128)S(1)} %get-tuple-element.17), channel_id=1, source_target_pairs={{0,124},{4,8},{8,4},{12,16},{16,12},{20,24},{24,20},{28,32},{32,28... | collective-permute-start | bytes 196616 | tf_op jit(solution)/shard_map/ppermute | solution.py:539
  4.9 0.0 copy-done.2
  4.9 4.8 %local.1 = (f32[64,128,128]{2,1,0:T(8,128)}, f32[64,32,128]{2,1,0:T(8,128)S(1)}, f32[64,8,128]{2,1,0:T(8,128)S(1)}) custom-call(f32[64,128,128]{2,1,0:T(8,128)S(1)} %bitcast.9, f32[64,32,128]{2,1,0:T(8,128)S(1)} %copy-done.1, f32[64,32,128]{2,1,0:T(8,128)S(1)} %copy-done.2), custom_call_target="tpu_custom_call" | custom-call | flops 67108864 | bytes 12582912 | tf_op jit(solution)/shard_map/local/pallas_call | solution.py:541
  9.6 0.0 collective-permute-done.got_a_ref.got_a_hbm
  9.7 0.0 collective-permute-done.1.got_b_ref.got_b_hbm
  9.7 0.0 copy-start.4
  9.7 0.1 edges.1
  9.7 1.7 %collective-permute-start.2 = (f32[64,4,128]{2,1,0:T(4,128)S(1)}, f32[64,4,128]{2,1,0:T(4,128)S(1)}, u32[]{:S(2)}, u32[]{:S(2)}) collective-permute-start(f32[64,4,128]{2,1,0:T(4,128)S(1)} %get-tuple-element.19), channel_id=1, source_target_pairs={{0,1},{1,0},{2,3},{3,2},{4,5},{5,4},{6,7},{7,6},{8,9},{9,8},{10,11... | collective-permute-start | bytes 393224 | tf_op jit(solution)/shard_map/ppermute | solution.py:565
  11.5 2.2 %collective-permute-start.3 = (f32[64,4,128]{2,1,0:T(4,128)S(1)}, f32[64,4,128]{2,1,0:T(4,128)S(1)}, u32[]{:S(2)}, u32[]{:S(2)}) collective-permute-start(f32[64,4,128]{2,1,0:T(4,128)S(1)} %get-tuple-element.20), channel_id=1, source_target_pairs={{0,3},{1,2},{2,1},{3,0},{4,7},{5,6},{6,5},{7,4},{8,11},{9,10},{10,... | collective-permute-start | bytes 393224 | tf_op jit(solution)/shard_map/ppermute | solution.py:566
  13.7 0.1 copy.11.trig_ref.trig_hbm
  13.8 0.0 copy-done.11
  13.8 1.8 %gains.1 = (f32[64,128]{1,0:T(8,128)S(1)}, bf16[2,128,128]{2,1,0:T(8,128)(2,1)S(1)}, f32[128,128]{1,0:T(8,128)S(1)}, bf16[256,256]{1,0:T(8,128)(2,1)S(1)}, bf16[256,128]{1,0:T(8,128)(2,1)S(1)}, /*index=5*/s32[1]{0:T(128)}) custom-call(f32[128,128]{1,0:T(8,128)S(1)} %copy-done.11, s32[1,128]{1,0:T(1,128)S(1)} %bitcast.11, s32[64,32]{1,0:T(8,128)S(1)} %copy.11.trig_ref.trig_hbm), custom_call_target="tpu_custom_call" | custom-call | flops 536870912 | bytes 1048576 | tf_op jit(solution)/shard_map/gains/pallas_call | solution.py:568
  15.6 0.0 collective-permute-done.2.got_c_hbm.got_c_ref
  15.6 0.9 %collective-permute-done.3.got_d_hbm.got_d_ref = f32[64,4,128]{2,1,0:T(4,128)S(1)} collective-permute-done((f32[64,4,128]{2,1,0:T(4,128)S(1)}, f32[64,4,128]{2,1,0:T(4,128)S(1)}, u32[]{:S(2)}, u32[]{:S(2)}) %collective-permute-start.3) | collective-permute-done | bytes 131104 | tf_op jit(solution)/shard_map/ppermute | solution.py:566
  16.5 2.6 %rain.1 = f32[128,128]{1,0:T(8,128)} custom-call(s32[128]{0:T(128)S(1)} %copy-done.10, s32[1]{0:T(128)} %get-tuple-element.15.bad_ref, f32[64,32,128]{2,1,0:T(8,128)S(1)} %get-tuple-element.24.tracer_ref, f32[128,128]{1,0:T(8,128)S(1)} %collective-permute-done.got_a_ref.got_a_hbm, f32[128,128]{1,0:T(8,128)S(1)} %collective-permute-done.1.got_b_ref.got_b_hbm, ...), custom_call_target="tpu_custom_call" | custom-call | flops 67108864 | bytes 2097152 | tf_op jit(solution)/shard_map/rain/pallas_call | solution.py:586
  19.1 11.1 %all-to-all-start = ((f32[128,1,128]{2,1,0:T(1,128)}), f32[128,1,128]{2,1,0:T(1,128)S(1)}, u32[]{:S(2)}, u32[]{:S(2)}) async-start(f32[128,1,128]{2,1,0:T(1,128)} %bitcast.4), calls=%async_computation | async-start | bytes 131072 | tf_op jit(solution)/shard_map/all_to_all | solution.py:597
  30.3 9.5 %mix.1 = f32[64,128,128]{2,1,0:T(8,128)} custom-call(s32[128]{0:T(128)} %cost_ref.3, s32[1]{0:T(128)} %get-tuple-element.15.bad_ref, f32[128,128]{1,0:T(8,128)} %mixing_hbm.1, s32[64,32]{1,0:T(8,128)} %copy-done.9, f32[128,128]{1,0:T(8,128)} %copy-done.3, f32[128,128]{1,0:T(8,128)} %copy-done.4, f32[64,4,128]{2,1,0:T(4,128)} %copy-done.5, ...), custom_call_target="tpu_custom_call" | custom-call | flops 4294967296 | bytes 10485760 | tf_op jit(solution)/shard_map/mix/pallas_call | solution.py:600
  39.8 0.1 all-to-all-done
  39.9 1.1 %gather.1 = f32[16,128]{1,0:T(8,128)} custom-call(f32[128,128]{1,0:T(8,128)S(1)} %bitcast.10), custom_call_target="tpu_custom_call" | custom-call | flops 1048576 | bytes 1048576 | tf_op jit(solution)/shard_map/gather/pallas_call | solution.py:627
  (22 shorter events, 0.0 us)
Async XLA Ops:
  0.6 4.2 %copy-start = (f32[64,32,4,128]{3,2,1,0:T(4,128)S(1)}, f32[64,32,4,128]{3,2,1,0:T(4,128)}, u32[]{:S(2)}) copy-start(f32[64,32,4,128]{3,2,1,0:T(4,128)} %param.7) | copy-start | bytes 12582916
  0.6 4.2 %copy-start.1 = (f32[64,32,128]{2,1,0:T(8,128)S(1)}, f32[64,32,128]{2,1,0:T(8,128)}, u32[]{:S(2)}) copy-start(f32[64,32,128]{2,1,0:T(8,128)} %wx.1) | copy-start | bytes 3145732
  0.6 4.2 %copy-start.2 = (f32[64,32,128]{2,1,0:T(8,128)S(1)}, f32[64,32,128]{2,1,0:T(8,128)}, u32[]{:S(2)}) copy-start(f32[64,32,128]{2,1,0:T(8,128)} %wy.1) | copy-start | bytes 3145732
  2.0 11.7 %copy-start.13 = (s32[64,32]{0,1:T(8,128)S(1)}, s32[64,32]{0,1:T(8,128)}, u32[]{:S(2)}) copy-start(s32[64,32]{0,1:T(8,128)} %param.11) | copy-start | bytes 24580
  2.0 11.7 %copy-start.11 = (f32[128,128]{1,0:T(8,128)S(1)}, f32[128,128]{1,0:T(8,128)}, u32[]{:S(2)}) copy-start(f32[128,128]{1,0:T(8,128)} %mixing_hbm.1) | copy-start | bytes 196612
  2.1 11.7 %copy-start.12 = (s32[128]{0:T(128)S(1)}, s32[128]{0:T(128)}, u32[]{:S(2)}) copy-start(s32[128]{0:T(128)} %param.13) | copy-start | bytes 1540
  2.1 7.6 %collective-permute-start = (f32[128,128]{1,0:T(8,128)S(1)}, f32[128,128]{1,0:T(8,128)S(1)}, u32[]{:S(2)}, u32[]{:S(2)}) collective-permute-start(f32[128,128]{1,0:T(8,128)S(1)} %get-tuple-element.16), channel_id=1, source_target_pairs={{0,4},{4,0},{8,12},{12,8},{16,20},{20,16},{24,28},{28,24},{32,36},... | collective-permute-start | bytes 196616 | tf_op jit(solution)/shard_map/ppermute | solution.py:538
  3.6 12.9 %copy-start.10 = (s32[128]{0:T(128)S(1)}, s32[128]{0:T(128)}, u32[]{:S(2)}) copy-start(s32[128]{0:T(128)} %cost_ref.3) | copy-start | bytes 1540
  3.6 6.1 %collective-permute-start.1 = (f32[128,128]{1,0:T(8,128)S(1)}, f32[128,128]{1,0:T(8,128)S(1)}, u32[]{:S(2)}, u32[]{:S(2)}) collective-permute-start(f32[128,128]{1,0:T(8,128)S(1)} %get-tuple-element.17), channel_id=1, source_target_pairs={{0,124},{4,8},{8,4},{12,16},{16,12},{20,24},{24,20},{28,32},{32,28... | collective-permute-start | bytes 196616 | tf_op jit(solution)/shard_map/ppermute | solution.py:539
  9.6 20.6 %copy-start.3 = (f32[128,128]{1,0:T(8,128)}, f32[128,128]{1,0:T(8,128)S(1)}, u32[]{:S(2)}) copy-start(f32[128,128]{1,0:T(8,128)S(1)} %collective-permute-done.got_a_ref.got_a_hbm) | copy-start | bytes 196612
  9.7 20.6 %copy-start.4 = (f32[128,128]{1,0:T(8,128)}, f32[128,128]{1,0:T(8,128)S(1)}, u32[]{:S(2)}) copy-start(f32[128,128]{1,0:T(8,128)S(1)} %collective-permute-done.1.got_b_ref.got_b_hbm) | copy-start | bytes 196612
  9.7 5.9 %collective-permute-start.2 = (f32[64,4,128]{2,1,0:T(4,128)S(1)}, f32[64,4,128]{2,1,0:T(4,128)S(1)}, u32[]{:S(2)}, u32[]{:S(2)}) collective-permute-start(f32[64,4,128]{2,1,0:T(4,128)S(1)} %get-tuple-element.19), channel_id=1, source_target_pairs={{0,1},{1,0},{2,3},{3,2},{4,5},{5,4},{6,7},{7,6},{8,9},{9,8},{10,11... | collective-permute-start | bytes 393224 | tf_op jit(solution)/shard_map/ppermute | solution.py:565
  11.5 5.0 %collective-permute-start.3 = (f32[64,4,128]{2,1,0:T(4,128)S(1)}, f32[64,4,128]{2,1,0:T(4,128)S(1)}, u32[]{:S(2)}, u32[]{:S(2)}) collective-permute-start(f32[64,4,128]{2,1,0:T(4,128)S(1)} %get-tuple-element.20), channel_id=1, source_target_pairs={{0,3},{1,2},{2,1},{3,0},{4,7},{5,6},{6,5},{7,4},{8,11},{9,10},{10,... | collective-permute-start | bytes 393224 | tf_op jit(solution)/shard_map/ppermute | solution.py:566
  13.8 16.5 %copy-start.9 = (s32[64,32]{1,0:T(8,128)}, s32[64,32]{1,0:T(8,128)S(1)}, u32[]{:S(2)}) copy-start(s32[64,32]{1,0:T(8,128)S(1)} %copy.11.trig_ref.trig_hbm) | copy-start | bytes 24580
  15.6 14.7 %copy-start.7 = (bf16[256,256]{1,0:T(8,128)(2,1)}, bf16[256,256]{1,0:T(8,128)(2,1)S(1)}, u32[]{:S(2)}) copy-start(bf16[256,256]{1,0:T(8,128)(2,1)S(1)} %get-tuple-element.21.first_hbm.first_ref) | copy-start | bytes 393220
  15.6 14.7 %copy-start.8 = (bf16[256,128]{1,0:T(8,128)(2,1)}, bf16[256,128]{1,0:T(8,128)(2,1)S(1)}, u32[]{:S(2)}) copy-start(bf16[256,128]{1,0:T(8,128)(2,1)S(1)} %get-tuple-element.22.second_hbm.second_ref) | copy-start | bytes 196612
  15.6 14.7 %copy-start.5 = (f32[64,4,128]{2,1,0:T(4,128)}, f32[64,4,128]{2,1,0:T(4,128)S(1)}, u32[]{:S(2)}) copy-start(f32[64,4,128]{2,1,0:T(4,128)S(1)} %collective-permute-done.2.got_c_hbm.got_c_ref) | copy-start | bytes 393220
  16.5 13.8 %copy-start.6 = (f32[64,4,128]{2,1,0:T(4,128)}, f32[64,4,128]{2,1,0:T(4,128)S(1)}, u32[]{:S(2)}) copy-start(f32[64,4,128]{2,1,0:T(4,128)S(1)} %collective-permute-done.3.got_d_hbm.got_d_ref) | copy-start | bytes 393220
  19.1 20.8 %all-to-all-start = ((f32[128,1,128]{2,1,0:T(1,128)}), f32[128,1,128]{2,1,0:T(1,128)S(1)}, u32[]{:S(2)}, u32[]{:S(2)}) async-start(f32[128,1,128]{2,1,0:T(1,128)} %bitcast.4), calls=%async_computation | async-start | bytes 131072 | tf_op jit(solution)/shard_map/all_to_all | solution.py:597

commit v2 on v1

--- a/solution.py
+++ b/solution.py
@@ -49,8 +49,7 @@
 
 
 def exact_pick(onehot, values):
-    high, mid, low = split3(values)
-    return mm(onehot, high) + mm(onehot, mid) + mm(onehot, low)
+    return mm(jnp.concatenate([onehot] * 3, axis=1), jnp.concatenate(split3(values), axis=0))
 
 
 def weights(high, mid, low):
@@ -72,7 +71,7 @@
     return lax.broadcasted_iota(jnp.int32, shape, dim)
 
 
-def gains_kernel(mixing_ref, dest_ref, trig_ref, gain_ref, onehot_ref, lanes_ref, first_ref, second_ref, bad_ref, sums):
+def gains_kernel(mixing_ref, dest_ref, cost_ref, trig_ref, table_ref, onehot_ref, lanes_ref, costs_ref, first_ref, second_ref, bad_ref, sums):
     square = mixing_ref[...]
     worst = jnp.max(jnp.abs(square))
     first_ref[...], second_ref[...] = weights(*split3(square.T))
@@ -93,30 +92,42 @@
         if k < 32:
             square = precise(*parts, *pair)
             worst = jnp.maximum(worst, jnp.max(jnp.abs(square)))
-    gain_ref[...] = 1.0 - sums[...]
-    bad_ref[0] = jnp.where(worst <= LIMIT, 0, 1).astype(jnp.int32)
-
-    groups = dest_ref.shape[1]
-    shape = (groups, groups)
-    dest_row = jnp.broadcast_to(dest_ref[...], shape)
-    diagonal = iota(shape, 0) == iota(shape, 1)
-    dest_col = jnp.sum(jnp.where(diagonal, dest_row, 0), axis=1, keepdims=True)
-    earlier = (dest_col == dest_row) & (iota(shape, 0) < iota(shape, 1))
-    within = jnp.sum(jnp.where(earlier, 1, 0), axis=0, keepdims=True)
-    at = dest_row == iota(shape, 0)
-    onehot_ref[0] = jnp.where(at & (within == 0), 1.0, 0.0).astype(BF16)
-    onehot_ref[1] = jnp.where(at & (within == 1), 1.0, 0.0).astype(BF16)
+    bad_ref[...] = jnp.full(bad_ref.shape, jnp.where(worst <= LIMIT, 0.0, 1.0), F32)
 
     px, py = trig_ref.shape
     half = py // 2
+    groups = 2 * px
+    shape = (groups, groups)
+    first_at, second_at = iota(shape, 0), iota(shape, 1)
+    number0 = 2 * (first_at % px) + first_at // px
+    number1 = 2 * (second_at % px) + second_at // px
+    diagonal = first_at == number1
+
+    def across(row):
+        return jnp.sum(jnp.where(first_at == second_at, row, 0), axis=1, keepdims=True)
+
+    def ordered(row_ref):
+        col = across(jnp.broadcast_to(row_ref[...], shape))
+        return jnp.sum(jnp.where(diagonal, col, 0), axis=0, keepdims=True)
+
+    dest_row = jnp.broadcast_to(ordered(dest_ref), shape)
+    dest_col = across(dest_row)
+    earlier = (dest_col == dest_row) & (number0 < number1)
+    within = jnp.sum(jnp.where(earlier, 1, 0), axis=0, keepdims=True)
+    at = dest_row == first_at
+    onehot_ref[0:groups] = jnp.where(at & (within == 0), 1.0, 0.0).astype(BF16)
+    onehot_ref[groups:2 * groups] = jnp.where(at & (within == 1), 1.0, 0.0).astype(BF16)
+
+    cost_col = across(jnp.broadcast_to(ordered(cost_ref), shape))
+    chosen = jnp.where(cost_col == iota((groups, MAXC), 1) + 1, 1.0, 0.0).astype(BF16)
+    table_ref[...] = exact_pick(chosen, 1.0 - sums[...])
+    costs_ref[...] = jnp.broadcast_to(cost_col, (groups, LEV)).astype(F32)
+
     wide = trig_ref[...].astype(F32).astype(BF16)
-    table = jnp.zeros((groups, LEV), F32)
+    lane = iota((py, LEV), 1)
     for h in range(2):
-        chosen = jnp.where(iota((groups, px), 0) == 2 * iota((groups, px), 1) + h, 1.0, 0.0).astype(BF16)
-        lane = iota((py, LEV), 1)
         placed = jnp.where((lane < 2 * half) & (lane % half + half * h == iota((py, LEV), 0)), 1.0, 0.0).astype(BF16)
-        table = table + mm(mm(chosen, wide).astype(BF16), placed)
-    lanes_ref[...] = table
+        lanes_ref[h * px:h * px + px] = mm(wide, placed)
 
 
 def half_coefs(first, second):
@@ -125,28 +136,38 @@
 
 def derivative_tables():
     deriv = -0.05 * gll_derivative()
-    g = [[float(np.float32(deriv[a, b])) for b in range(4)] for a in range(4)]
-    low = [half_coefs(g[0][0], g[1][1]), half_coefs(g[0][1], g[1][0]), half_coefs(g[0][2], g[1][3]), half_coefs(g[0][3], g[1][2])]
-    high = [half_coefs(g[2][0], g[3][1]), half_coefs(g[2][1], g[3][0]), half_coefs(g[2][2], g[3][3]), half_coefs(g[2][3], g[3][2])]
-    return g, low, high
+    even = [float(np.float32(0.5 * (deriv[a, 0] + deriv[a, 3]))) for a in range(2)]
+    odd = [[float(np.float32(0.5 * (deriv[a, b] - deriv[a, 3 - b]))) for b in range(2)] for a in range(2)]
+    return even, odd
 
 
 def tendency(k, points, load, load_x, load_y, store):
-    g, low, high = derivative_tables()
+    even, odd = derivative_tables()
+    c_even = half_coefs(even[0], -even[1])
+    c_odd, c_cross = half_coefs(odd[0][0], odd[1][1]), half_coefs(odd[0][1], odd[1][0])
     lower = iota((8, LEV), 0) < 4
     v = [[load(a, 16 * k + 8 * h) for h in range(2)] for a in range(NP)]
+    along_x = []
+    for h in range(2):
+        d0, d1 = v[0][h] - v[3][h], v[1][h] - v[2][h]
+        mean = (v[0][h] + v[3][h]) - (v[1][h] + v[2][h])
+        p0, p1 = even[0] * mean, even[1] * mean
+        q0, q1 = odd[0][0] * d0 + odd[0][1] * d1, odd[1][0] * d0 + odd[1][1] * d1
+        along_x.append((q0 + p0, q1 + p1, q1 - p1, q0 - p0))
     for a in points:
-        r = [pltpu.roll(v[a][h], 4, axis=0) for h in range(2)]
-        for h, coefs in ((0, low), (1, high)):
-            along_y = (coefs[0] * v[a][0] + coefs[1] * r[0]) + (coefs[2] * v[a][1] + coefs[3] * r[1])
-            along_x = (g[a][0] * v[0][h] + g[a][1] * v[1][h]) + (g[a][2] * v[2][h] + g[a][3] * v[3][h])
+        r1 = pltpu.roll(v[a][1], 4, axis=0)
+        add, sub = v[a][0] + r1, v[a][0] - r1
+        odds = c_odd * sub + c_cross * pltpu.roll(sub, 4, axis=0)
+        evens = c_even * (add - pltpu.roll(add, 4, axis=0))
+        along_y = (odds + evens, pltpu.roll(odds - evens, 4, axis=0))
+        for h in range(2):
             y = 4 * k + 2 * h
             wx = jnp.where(lower, load_x(a, y), load_x(a, y + 1))
             wy = jnp.where(lower, load_y(a, y), load_y(a, y + 1))
-            store(a, 16 * k + 8 * h, wx * along_x + wy * along_y)
-
-
-def sides_kernel(state_hbm, wx_hbm, wy_hbm, send_a_ref, send_b_ref, state, wx, wy, ends, sems):
+            store(a, 16 * k + 8 * h, wx * along_x[h][a] + wy * along_y[h])
+
+
+def sides_kernel(state_hbm, wx_hbm, wy_hbm, send_b_ref, send_a_ref, state, wx, wy, ends, sems):
     even = lax.axis_index("elem") % 2 == 0
     px = state_hbm.shape[0]
     copies = []
@@ -236,7 +257,7 @@
         out_copy(e).wait()
 
 
-def edge_kernel(edge_ref, got_a_ref, got_b_ref, send_c_ref, send_d_ref):
+def edge_kernel(edge_ref, got_b_ref, got_a_ref, send_d_ref, send_c_ref, both):
     even = lax.axis_index("elem") % 2 == 0
     even_y = lax.axis_index("blk") % 2 == 0
     px = edge_ref.shape[0]
@@ -245,13 +266,14 @@
     before = jnp.where(even, got_b_ref[...], got_a_ref[...])
     after = jnp.where(even, got_a_ref[...], got_b_ref[...])
     for x in range(px):
-        both = edge_ref[x]
-        if x == 0:
-            both = both + 0.5 * jnp.where(lower, before[0:8], before[rows - 8:rows])
-        if x == px - 1:
-            both = both + 0.5 * jnp.where(lower, after[0:8], after[rows - 8:rows])
-        send_c_ref[x] = jnp.where(even_y, both[4:8], both[0:4])
-        send_d_ref[x] = jnp.where(even_y, both[0:4], both[4:8])
+        both[8 * x:8 * x + 8, :] = edge_ref[x]
+    for x, side in ((0, before), (px - 1, after)):
+        both[8 * x:8 * x + 8, :] = edge_ref[x] + 0.5 * jnp.where(lower, side[0:8], side[rows - 8:rows])
+    for t in range(NT):
+        first = both[pl.ds(t, px, stride=8), :]
+        final = both[pl.ds(NT + t, px, stride=8), :]
+        send_c_ref[t * px:t * px + px, :] = jnp.where(even_y, final, first)
+        send_d_ref[t * px:t * px + px, :] = jnp.where(even_y, first, final)
 
 
 def side_shares(even, got_a_ref, got_b_ref, rows):
@@ -260,71 +282,95 @@
     return smooth_rows(before, None, None), smooth_rows(after, None, None)
 
 
-def rain_kernel(cost_ref, bad_ref, tracer_ref, got_a_ref, got_b_ref, got_c_ref, got_d_ref, mask_ref, gain_ref, onehot_ref, first_ref, second_ref, out_ref, rain_ref, side_ref):
+def rain_place(half):
+    lane = iota((half, LEV), 1)
+    return (lane < 2 * half) & (lane % half == iota((half, LEV), 0))
+
+
+def rain_row(part, place):
+    sums = jnp.sum(part, axis=1, keepdims=True) * 0.125
+    return jnp.sum(jnp.where(place, sums, 0.0), axis=0, keepdims=True)
+
+
+def early_rain_kernel(tracer_ref, got_a_ref, got_b_ref, table_ref, rain_ref, side_ref):
     px, py, _ = tracer_ref.shape
     half = py // 2
     rows = py * NT
-    even_y = lax.axis_index("blk") % 2 == 0
     for s, side in enumerate(side_shares(lax.axis_index("elem") % 2 == 0, got_a_ref, got_b_ref, rows)):
         for i, value in enumerate(side):
             side_ref[s, 8 * i:8 * i + 8, :] = value
-    at_first = iota((half, LEV), 0) == 0
-    at_final = iota((half, LEV), 0) == half - 1
-
-    def advanced(x):
-        up = 0.5 * jnp.where(even_y, got_d_ref[x, 1:2, :], got_c_ref[x, 1:2, :])
-        down = 0.5 * jnp.where(even_y, got_c_ref[x, 1:2, :], got_d_ref[x, 1:2, :])
-        low = tracer_ref[x, 0:half, :] + jnp.where(at_first, up, 0.0)
-        high = tracer_ref[x, half:py, :] + jnp.where(at_final, down, 0.0)
-        if isinstance(x, int):
-            extra = side_ref[0 if x == 0 else 1, pl.ds(1, py, stride=NT), :]
-            return low + extra[0:half], high + extra[half:py]
-        return low, high
-
-    place = (iota((half, LEV), 1) < 2 * half) & (iota((half, LEV), 1) % half == iota((half, LEV), 0))
-
-    def weigh(x, part, h):
-        return part * gain_ref[pl.ds(cost_ref[2 * x + h] - 1, 1), :]
-
-    def step_by_step(x, part, h):
-        return part - repeated(part, cost_ref[2 * x + h], first_ref, second_ref)
-
-    def fill(rule, unroll):
-        def one(x):
-            for h, part in enumerate(advanced(x)):
-                sums = jnp.sum(rule(x, part, h), axis=1, keepdims=True) * 0.125
-                rain_ref[pl.ds(2 * x + h, 1), :] = jnp.sum(jnp.where(place, sums, 0.0), axis=0, keepdims=True)
-
-        one(0)
-        one(px - 1)
-
-        def step(x, carry):
-            one(x)
+    place = rain_place(half)
+
+    def one(x, extra):
+        for h in range(2):
+            part = tracer_ref[x, half * h:half * h + half, :]
+            if extra is not None:
+                part = part + extra[half * h:half * h + half]
+            at = pl.ds(h * px + x, 1)
+            rain_ref[at, :] = rain_row(part * table_ref[at, :], place)
+
+    for x in range(px):
+        side = {0: 0, px - 1: 1}.get(x)
+        one(x, None if side is None else side_ref[side, pl.ds(1, py, stride=NT), :])
+
+
+def rain_kernel(costs_ref, bad_ref, tracer_ref, got_a_ref, got_b_ref, got_c_ref, got_d_ref, early_ref, table_ref, lanes_ref, onehot_ref, first_ref, second_ref, out_ref, rain_ref, side_ref):
+    px, py, _ = tracer_ref.shape
+    half = py // 2
+    rows = py * NT
+    groups = 2 * px
+    even_y = lax.axis_index("blk") % 2 == 0
+    up = 0.5 * jnp.where(even_y, got_d_ref[px:2 * px, :], got_c_ref[px:2 * px, :])
+    down = 0.5 * jnp.where(even_y, got_c_ref[px:2 * px, :], got_d_ref[px:2 * px, :])
+
+    lane = iota((groups, LEV), 1)
+
+    def send(rain):
+        values = jnp.where(lane == 2 * half, 1.0, jnp.where(lanes_ref[...] > 0.5, rain, 0.0))
+        picked = exact_pick(onehot_ref[...], values)
+        first, second = picked[:groups], picked[groups:]
+        out_ref[...] = jnp.where(lane < half, first, jnp.where(lane < 2 * half, second, first + second))
+
+    sums = jnp.sum(jnp.concatenate([up, down], axis=0) * table_ref[...], axis=1, keepdims=True) * 0.125
+    column = jnp.where(iota((groups, LEV), 0) < px, 0, half - 1)
+    send(early_ref[...] + jnp.where((lane == column) | (lane == column + half), sums, 0.0))
+    bad = jnp.max(bad_ref[...]) > 0.5
+
+    @pl.when(bad)
+    def _():
+        for s, side in enumerate(side_shares(lax.axis_index("elem") % 2 == 0, got_a_ref, got_b_ref, rows)):
+            for i, value in enumerate(side):
+                side_ref[s, 8 * i:8 * i + 8, :] = value
+        rain_ref[0:px, :] = up
+        rain_ref[px:2 * px, :] = down
+        place = rain_place(half)
+        row = iota((half, LEV), 0)
+
+        def one(x, carry):
+            near = jnp.where(x == 0, 1.0, 0.0).astype(F32)
+            far = jnp.where(x == px - 1, 1.0, 0.0).astype(F32)
+            for h, at in ((0, 0), (1, half - 1)):
+                def side(s):
+                    return side_ref[s, pl.ds(1 + half * NT * h, half, stride=NT), :]
+
+                here = pl.ds(h * px + x, 1)
+                part = tracer_ref[x, half * h:half * h + half, :] + (near * side(0) + far * side(1))
+                part = part + jnp.where(row == at, rain_ref[here, :], 0.0)
+                done = repeated(part, jnp.max(costs_ref[here, :]).astype(jnp.int32), first_ref, second_ref)
+                rain_ref[here, :] = rain_row(part - done, place)
             return carry
 
-        lax.fori_loop(1, px - 1, step, 0, unroll=unroll)
-
-    @pl.when(bad_ref[0] == 0)
-    def _():
-        fill(weigh, 31)
-
-    @pl.when(bad_ref[0] != 0)
-    def _():
-        fill(step_by_step, 1)
-
-    lane = iota(out_ref.shape, 1)
-    values = jnp.where(lane == 2 * half, 1.0, jnp.where(mask_ref[...] > 0.5, rain_ref[...], 0.0))
-    first = exact_pick(onehot_ref[0], values)
-    second = exact_pick(onehot_ref[1], values)
-    out_ref[...] = jnp.where(lane < half, first, jnp.where(lane < 2 * half, second, first + second))
-
-
-def mix_kernel(cost_ref, bad_ref, mixing_hbm, trig_hbm, got_a_hbm, got_b_hbm, got_c_hbm, got_d_hbm, first_hbm, second_hbm, adv_hbm, new_hbm, adv, new, powers, mixing_ref, trig_ref, got_a_ref, got_b_ref, got_c_ref, got_d_ref, first_ref, second_ref, mask_ref, sems, out_sems, small_sems):
+        lax.fori_loop(0, px, one, 0)
+        send(rain_ref[...])
+
+
+def mix_kernel(cost_hbm, bad_hbm, mixing_hbm, trig_hbm, got_a_hbm, got_b_hbm, got_c_hbm, got_d_hbm, first_hbm, second_hbm, adv_hbm, new_hbm, adv, new, powers, cost_ref, bad_ref, mixing_ref, trig_ref, got_a_ref, got_b_ref, got_c_ref, got_d_ref, first_ref, second_ref, mask_ref, sems, out_sems, small_sems):
     px, rows, _ = adv.shape
     py = rows // NT
     half = rows // 2
     chunks = sems.shape[0]
     size = px // chunks
+    out = px // out_sems.shape[0]
     even_y = lax.axis_index("blk") % 2 == 0
     lower = iota((8, LEV), 0) < 4
 
@@ -332,13 +378,15 @@
         return pltpu.make_async_copy(adv_hbm.at[pl.ds(i * size, size)], adv.at[pl.ds(i * size, size)], sems.at[i])
 
     def out_copy(i):
-        return pltpu.make_async_copy(new.at[pl.ds(i * size, size)], new_hbm.at[pl.ds(i * size, size)], out_sems.at[i])
+        return pltpu.make_async_copy(new.at[pl.ds(i * out, out)], new_hbm.at[pl.ds(i * out, out)], out_sems.at[i])
 
     small = [
         pltpu.make_async_copy(src, dst, small_sems.at[i])
         for i, (src, dst) in enumerate(
             (
                 (mixing_hbm, mixing_ref),
+                (bad_hbm, bad_ref),
+                (cost_hbm, cost_ref),
                 (trig_hbm, trig_ref),
                 (got_a_hbm, got_a_ref),
                 (got_b_hbm, got_b_ref),
@@ -354,8 +402,11 @@
     for i in range(chunks):
         in_copy(i).start()
     small[0].wait()
-
-    @pl.when(bad_ref[0] == 0)
+    small[1].wait()
+    bad = jnp.max(bad_ref[...]) > 0.5
+    good = jnp.logical_not(bad)
+
+    @pl.when(good)
     def _():
         powers[0] = jnp.concatenate(split3(mixing_ref[...].T), axis=1)
 
@@ -382,7 +433,7 @@
 
             lax.fori_loop(0, k, later, 0, unroll=8)
 
-    for copy in small[1:]:
+    for copy in small[2:]:
         copy.wait()
     trig = jnp.concatenate([trig_ref[...].astype(F32), jnp.zeros((LEV - px, py), F32)], axis=0).T
     spread = jnp.where(iota((rows, py), 0) // NT == iota((rows, py), 1), 1.0, 0.0).astype(BF16)
@@ -396,10 +447,11 @@
 
     def edged(x, h):
         start = adv[x, half * h:half * h + half, :]
+        at = pl.ds(x, NT, stride=px)
         if h == 0:
-            add = 0.5 * jnp.where(even_y, got_d_ref[x], got_c_ref[x])
+            add = 0.5 * jnp.where(even_y, got_d_ref[at, :], got_c_ref[at, :])
             return jnp.concatenate([start[0:8] + jnp.where(lower, jnp.concatenate([add, add], axis=0), 0.0), start[8:]], axis=0)
-        add = 0.5 * jnp.where(even_y, got_c_ref[x], got_d_ref[x])
+        add = 0.5 * jnp.where(even_y, got_c_ref[at, :], got_d_ref[at, :])
         return jnp.concatenate([start[:half - 8], start[half - 8:] + jnp.where(lower, 0.0, jnp.concatenate([add, add], axis=0))], axis=0)
 
     def powered(x, h, start):
@@ -421,19 +473,20 @@
         def _():
             in_copy(i).wait()
 
-    @pl.when(bad_ref[0] == 0)
+    @pl.when(good)
     def _():
         def chunk(i, carry):
             arrive(i)
             rolled = pltpu.roll(mask_ref[...], lax.rem(LEV - i * size, LEV), axis=1)
             for a in range(size):
                 one(powered, i * size + a, jnp.broadcast_to(rolled[:, a:a + 1], (rows, LEV)))
-            out_copy(i).start()
+                if a % out == out - 1:
+                    out_copy(i * (size // out) + a // out).start()
             return carry
 
         lax.fori_loop(0, chunks, chunk, 0)
 
-    @pl.when(bad_ref[0] != 0)
+    @pl.when(bad)
     def _():
         def chunk(i, carry):
             arrive(i)
@@ -445,12 +498,13 @@
                 return carry
 
             lax.fori_loop(0, size, column, 0)
-            out_copy(i).start()
+            for j in range(size // out):
+                out_copy(i * (size // out) + j).start()
             return carry
 
         lax.fori_loop(0, chunks, chunk, 0)
 
-    for i in range(chunks):
+    for i in range(px // out):
         out_copy(i).wait()
 
 
@@ -465,27 +519,18 @@
     per = LEV // half
     rows = size[0] // per
     slot = (iota(size, 0) % rows) * per + iota(size, 0) // rows
-    pick0 = jnp.where((slot == start) & (count > 0), 1.0, 0.0).astype(BF16)
-    pick1 = jnp.where((slot == start + 1) & (count > 1), 1.0, 0.0).astype(BF16)
-    tile0 = jnp.where(iota(size, 0) == iota(size, 1) % half, 1.0, 0.0).astype(BF16)
-    tile1 = jnp.where(iota(size, 0) == iota(size, 1) % half + half, 1.0, 0.0).astype(BF16)
-
-    def tiled(tile):
-        high, mid, low = split3(got)
-        return mm(high, tile).astype(BF16), mm(mid, tile).astype(BF16), mm(low, tile).astype(BF16)
-
-    total = jnp.zeros(size, F32)
-    for pick, tile in ((pick0, tile0), (pick1, tile1)):
-        high, mid, low = tiled(tile)
-        total = total + ((mm(pick, high) + mm(pick, mid)) + mm(pick, low))
+    pick0 = jnp.where((slot == start) & (count > 0), 1.0, 0.0)
+    pick1 = jnp.where((slot == start + 1) & (count > 1), 1.0, 0.0)
+    picked = exact_pick(jnp.concatenate([pick0, pick1], axis=0).astype(BF16), got)
     lane = iota((rows, LEV), 1)
-    out = jnp.zeros((rows, LEV), F32)
-    for q in range(per):
-        out = jnp.where(lane // half == q, total[q * rows:(q + 1) * rows], out)
+    first, second = picked[:size[0]], pltpu.roll(picked[size[0]:], LEV - half, axis=1)
+    total = jnp.where(iota(size, 1) < half, first + second, 0.0)
+    out = total[0:rows]
+    for q in range(1, per):
+        out = jnp.where(lane // half == q, pltpu.roll(total[q * rows:(q + 1) * rows], half * q, axis=1), out)
     rain_ref[...] = out
 
 
-SMEM = pl.BlockSpec(memory_space=pltpu.SMEM)
 VMEM = pl.BlockSpec(memory_space=pltpu.VMEM)
 HBM = pl.BlockSpec(memory_space=pltpu.HBM)
 
@@ -514,7 +559,7 @@
     def kept(x):
         return pltpu.with_memory_space_constraint(x, pltpu.HBM)
 
-    send_a, send_b = pl.pallas_call(
+    send_b, send_a = pl.pallas_call(
         sides_kernel,
         out_shape=(struct(rows, lev),) * 2,
         in_specs=[HBM] * 3,
@@ -535,8 +580,8 @@
     pair_b = [(i, (i - 1 if i % 2 == 0 else i + 1) % n_elem) for i in range(n_elem)]
     pair_c = [(j, j ^ 1) for j in range(n_blk)]
     pair_d = [(j, (j - 1 if j % 2 == 0 else j + 1) % n_blk) for j in range(n_blk)]
+    got_b = lax.ppermute(send_b, "elem", pair_b)
     got_a = lax.ppermute(send_a, "elem", pair_a)
-    got_b = lax.ppermute(send_b, "elem", pair_b)
 
     local, tracer, edges = pl.pallas_call(
         local_kernel,
@@ -553,46 +598,59 @@
         name="local",
     )(slabs, wind_x, wind_y)
 
-    send_c, send_d = pl.pallas_call(
+    send_d, send_c = pl.pallas_call(
         edge_kernel,
-        out_shape=(struct(px, nt, lev),) * 2,
+        out_shape=(struct(nt * px, lev),) * 2,
         in_specs=[VMEM, VMEM, VMEM],
         out_specs=(VMEM, VMEM),
+        scratch_shapes=[pltpu.VMEM((8 * px, lev), F32)],
         compiler_params=params(8),
         cost_estimate=cost(MIB, MIB),
         name="edges",
-    )(edges, got_a, got_b)
+    )(edges, got_b, got_a)
+    got_d = lax.ppermute(send_d, "blk", pair_d)
     got_c = lax.ppermute(send_c, "blk", pair_c)
-    got_d = lax.ppermute(send_d, "blk", pair_d)
-
-    gains, onehots, lanes, first, second, bad = pl.pallas_call(
+
+    table, onehots, lanes, costs, first, second, bad = pl.pallas_call(
         gains_kernel,
         out_shape=(
-            struct(MAXC, lev),
-            struct(2, groups, groups, dtype=BF16),
+            struct(groups, lev),
+            struct(2 * groups, groups, dtype=BF16),
+            struct(groups, lev),
             struct(groups, lev),
             struct(2 * lev, 2 * lev, dtype=BF16),
             struct(2 * lev, lev, dtype=BF16),
-            struct(1, dtype=jnp.int32),
+            struct(8, lev),
         ),
-        in_specs=[VMEM, VMEM, VMEM],
-        out_specs=(VMEM, VMEM, VMEM, VMEM, VMEM, SMEM),
+        in_specs=[VMEM] * 4,
+        out_specs=(VMEM,) * 7,
         scratch_shapes=[pltpu.VMEM((MAXC, lev), F32)],
         compiler_params=params(8),
         cost_estimate=cost(512 * MIB, MIB),
         name="gains",
-    )(mixing, destinations.reshape(1, groups), triggers)
+    )(mixing, destinations.reshape(1, groups), group_costs.reshape(1, groups), triggers)
+
+    early = pl.pallas_call(
+        early_rain_kernel,
+        out_shape=struct(groups, lev),
+        in_specs=[VMEM] * 4,
+        out_specs=VMEM,
+        scratch_shapes=[pltpu.VMEM((2, rows, lev), F32)],
+        compiler_params=params(8),
+        cost_estimate=cost(512 * MIB, MIB),
+        name="early_rain",
+    )(tracer, got_a, got_b, table)
 
     outgoing = pl.pallas_call(
         rain_kernel,
         out_shape=struct(groups, lev),
-        in_specs=[SMEM, SMEM] + [VMEM] * 10,
+        in_specs=[VMEM] * 13,
         out_specs=VMEM,
         scratch_shapes=[pltpu.VMEM((groups, lev), F32), pltpu.VMEM((2, rows, lev), F32)],
         compiler_params=params(12),
         cost_estimate=cost(64 * MIB, 2 * MIB),
         name="rain",
-    )(group_costs, bad, tracer, got_a, got_b, got_c, got_d, lanes, gains, onehots, first, second)
+    )(costs, bad, tracer, got_a, got_b, got_c, got_d, early, table, lanes, onehots, first, second)
 
     incoming = lax.all_to_all(outgoing, ("elem", "blk"), split_axis=0, concat_axis=0, tiled=True)
 
@@ -600,24 +658,26 @@
     new = pl.pallas_call(
         mix_kernel,
         out_shape=struct(px, rows, lev),
-        in_specs=[SMEM, SMEM] + [HBM] * 9,
+        in_specs=[HBM] * 11,
         out_specs=HBM,
         scratch_shapes=[
             pltpu.VMEM((px, rows, lev), F32),
             pltpu.VMEM((px, rows, lev), F32),
             pltpu.VMEM((MAXC, lev, 3 * lev), BF16),
+            pltpu.SMEM((groups,), jnp.int32),
+            pltpu.VMEM((8, lev), F32),
             pltpu.VMEM((lev, lev), F32),
             pltpu.VMEM((px, py), jnp.int32),
             pltpu.VMEM((rows, lev), F32),
             pltpu.VMEM((rows, lev), F32),
-            pltpu.VMEM((px, nt, lev), F32),
-            pltpu.VMEM((px, nt, lev), F32),
+            pltpu.VMEM((nt * px, lev), F32),
+            pltpu.VMEM((nt * px, lev), F32),
             pltpu.VMEM((2 * lev, 2 * lev), BF16),
             pltpu.VMEM((2 * lev, lev), BF16),
             pltpu.VMEM((rows, lev), F32),
             pltpu.SemaphoreType.DMA((chunks,)),
-            pltpu.SemaphoreType.DMA((chunks,)),
-            pltpu.SemaphoreType.DMA((8,)),
+            pltpu.SemaphoreType.DMA((2 * chunks,)),
+            pltpu.SemaphoreType.DMA((10,)),
         ],
         compiler_params=params(60),
         cost_estimate=cost(4096 * MIB, 10 * MIB),

time: 41.1 us -> 38.4 us (0.934)
  Pallas kernels: 21.1 us -> 17.6 us
  waiting for transfers between devices: 0.98 us -> 2.21 us
  starting transfers between devices: 17.9 us -> 17.4 us
    pallas_call x4 -> x5, Pallas kernels: 13.9 us -> 10.9 us  [the longest x1 8.23 us: body(): pl.pallas_call(mix_kernel, out_shape=struct(px, rows, lev), in_specs=[HBM...]
    all_to_all x1, waiting for transfers between devices: 0.1 us -> 1.32 us  [body(): lax.all_to_all(outgoing, ('elem', 'blk'), split_axis=0, concat_axis=0, ti...]
    pallas_call x1, Pallas kernels: 4.77 us -> 4.21 us  [body(): pl.pallas_call(local_kernel, out_shape=(pltpu.HBM((px, rows, lev), F32),...]
    all_to_all x1, starting transfers between devices: 11.1 us -> 10.7 us  [body(): lax.all_to_all(outgoing, ('elem', 'blk'), split_axis=0, concat_axis=0, ti...]
  transfers between devices with their start and end apart: 5 -> 5, of which waited for: 2 -> 2; matrix products, arithmetic and copies ran while one was open for 0% -> 0% of each run, Pallas kernels for 39% -> 37%
where the time goes in v2:
time: 38.4 us; the launch traced here: 38.2 us
  Pallas kernels  17.6 us (46%)
  starting transfers between devices  17.4 us (45%)
  waiting for transfers between devices  2.21 us (6%)
  between operations  0.9 us (2%)
    all_to_all x1, starting transfers between devices, body(): lax.all_to_all(outgoing, ('elem', 'blk'), split_axis=0, concat_axis=0, ti...  10.7 us
    pallas_call x1, Pallas kernels, body(): pl.pallas_call(mix_kernel, out_shape=struct(px, rows, lev), in_specs=[HBM...  8.23 us
    pallas_call x1, Pallas kernels, body(): pl.pallas_call(local_kernel, out_shape=(pltpu.HBM((px, rows, lev), F32),...  4.21 us
    ppermute x1, starting transfers between devices, body(): got_d = lax.ppermute(send_d, 'blk', pair_d)  2.24 us
    ppermute x1, starting transfers between devices, body(): got_c = lax.ppermute(send_c, 'blk', pair_c)  1.72 us
    ppermute x1, starting transfers between devices, body(): got_a = lax.ppermute(send_a, 'elem', pair_a)  1.5 us
    pallas_call x1, Pallas kernels, body(): pl.pallas_call(sides_kernel, out_shape=(struct(rows, lev),) * 2, in_specs...  1.37 us
    pallas_call x1, Pallas kernels, body(): pl.pallas_call(gains_kernel, out_shape=(struct(groups, lev), struct(2 * g...  1.36 us
  transfers between devices with their start and end apart: 5, of which 2 were waited for; matrix products, arithmetic and copies ran while one was open for 0% of the time, Pallas kernels for 37%

profile of v2, /device:TPU:1, one launch (start us, length us, event | category | flops | bytes accessed | tf_op | source)
XLA Modules:
  0.0 38.2 jit_solution(5549949874862074501)
XLA Ops:
  0.7 1.4 %sides.1 = (f32[128,128]{1,0:T(8,128)S(1)}, f32[128,128]{1,0:T(8,128)S(1)}) custom-call(f32[64,128,128]{2,1,0:T(8,128)} %bitcast.9, f32[64,32,128]{2,1,0:T(8,128)} %wx.1, f32[64,32,128]{2,1,0:T(8,128)} %wy.1), custom_call_target="tpu_custom_call" | custom-call | flops 2097152 | bytes 1048576 | tf_op jit(solution)/shard_map/sides/pallas_call | solution.py:562
  2.0 0.0 copy-start.14
  2.0 0.0 copy-start.11
  2.1 0.0 copy-start.12
  2.1 0.0 copy-start.13
  2.1 1.5 %collective-permute-start = (f32[128,128]{1,0:T(8,128)S(1)}, f32[128,128]{1,0:T(8,128)S(1)}, u32[]{:S(2)}, u32[]{:S(2)}) collective-permute-start(f32[128,128]{1,0:T(8,128)S(1)} %get-tuple-element.17), channel_id=1, source_target_pairs={{0,4},{4,0},{8,12},{12,8},{16,20},{20,16},{24,28},{28,24},{32,36},... | collective-permute-start | bytes 196616 | tf_op jit(solution)/shard_map/ppermute | solution.py:584
  3.6 1.3 %collective-permute-start.1 = (f32[128,128]{1,0:T(8,128)S(1)}, f32[128,128]{1,0:T(8,128)S(1)}, u32[]{:S(2)}, u32[]{:S(2)}) collective-permute-start(f32[128,128]{1,0:T(8,128)S(1)} %get-tuple-element.18), channel_id=1, source_target_pairs={{0,124},{4,8},{8,4},{12,16},{16,12},{20,24},{24,20},{28,32},{32,28... | collective-permute-start | bytes 196616 | tf_op jit(solution)/shard_map/ppermute | solution.py:583
  4.9 4.2 %local.1 = (f32[64,128,128]{2,1,0:T(8,128)}, f32[64,32,128]{2,1,0:T(8,128)S(1)}, f32[64,8,128]{2,1,0:T(8,128)S(1)}) custom-call(f32[64,128,128]{2,1,0:T(8,128)S(1)} %bitcast.10, f32[64,32,128]{2,1,0:T(8,128)S(1)} %copy-done.1, f32[64,32,128]{2,1,0:T(8,128)S(1)} %copy-done.2), custom_call_target="tpu_custom_call" | custom-call | flops 67108864 | bytes 12582912 | tf_op jit(solution)/shard_map/local/pallas_call | solution.py:586
  9.1 0.0 collective-permute-done.got_a_ref.got_a_hbm
  9.1 0.0 collective-permute-done.1.got_b_ref.got_b_hbm
  9.1 0.1 edges.1
  9.2 1.7 %collective-permute-start.2 = (f32[256,128]{1,0:T(8,128)S(1)}, f32[256,128]{1,0:T(8,128)S(1)}, u32[]{:S(2)}, u32[]{:S(2)}) collective-permute-start(f32[256,128]{1,0:T(8,128)S(1)} %get-tuple-element.20), channel_id=1, source_target_pairs={{0,1},{1,0},{2,3},{3,2},{4,5},{5,4},{6,7},{7,6},{8,9},{9,8},{10,11... | collective-permute-start | bytes 393224 | tf_op jit(solution)/shard_map/ppermute | solution.py:612
  10.9 2.2 %collective-permute-start.3 = (f32[256,128]{1,0:T(8,128)S(1)}, f32[256,128]{1,0:T(8,128)S(1)}, u32[]{:S(2)}, u32[]{:S(2)}) collective-permute-start(f32[256,128]{1,0:T(8,128)S(1)} %get-tuple-element.21), channel_id=1, source_target_pairs={{0,3},{1,2},{2,1},{3,0},{4,7},{5,6},{6,5},{7,4},{8,11},{9,10},{10,... | collective-permute-start | bytes 393224 | tf_op jit(solution)/shard_map/ppermute | solution.py:611
  13.2 0.1 copy.11.trig_ref.trig_hbm
  13.3 1.4 %gains.1 = (f32[128,128]{1,0:T(8,128)S(1)}, bf16[256,128]{1,0:T(8,128)(2,1)S(1)}, f32[128,128]{1,0:T(8,128)S(1)}, f32[128,128]{1,0:T(8,128)S(1)}, bf16[256,256]{...) custom-call(f32[128,128]{1,0:T(8,128)S(1)} %copy-done.11, s32[1,128]{1,0:T(1,128)S(1)} %bitcast.12, ...), custom_call_target="tpu_custom_call" | custom-call | flops 536870912 | bytes 1048576 | tf_op jit(solution)/shard_map/gains/pallas_call | solution.py:614
  14.7 0.0 copy-start.10
  14.7 0.4 early_rain.1.early_ref
  15.0 0.0 collective-permute-done.2.got_c_hbm.got_c_ref
  15.1 0.9 %collective-permute-done.3.got_d_hbm.got_d_ref = f32[256,128]{1,0:T(8,128)S(1)} collective-permute-done((f32[256,128]{1,0:T(8,128)S(1)}, f32[256,128]{1,0:T(8,128)S(1)}, u32[]{:S(2)}, u32[]{:S(2)}) %collective-permute-start.3) | collective-permute-done | bytes 131104 | tf_op jit(solution)/shard_map/ppermute | solution.py:611
  15.9 0.9 %rain.1 = f32[128,128]{1,0:T(8,128)} custom-call(f32[128,128]{1,0:T(8,128)S(1)} %get-tuple-element.25.costs_ref, f32[8,128]{1,0:T(8,128)S(1)} %get-tuple-element.16.bad_hbm.bad_ref, f32[64,32,128]{2,1,0:T(8,128)S(1)} %get-tuple-element.26.tracer_ref, f32[128,128]{1,0:T(8,128)S(1)} %collective-permute-done.got_a_ref.got_a_hbm, ...), custom_call_target="tpu_custom_call" | custom-call | flops 67108864 | bytes 2097152 | tf_op jit(solution)/shard_map/rain/pallas_call | solution.py:644
  16.9 10.7 %all-to-all-start = ((f32[128,1,128]{2,1,0:T(1,128)}), f32[128,1,128]{2,1,0:T(1,128)S(1)}, u32[]{:S(2)}, u32[]{:S(2)}) async-start(f32[128,1,128]{2,1,0:T(1,128)} %bitcast.5), calls=%async_computation | async-start | bytes 131072 | tf_op jit(solution)/shard_map/all_to_all | solution.py:655
  27.6 8.2 %mix.1 = f32[64,128,128]{2,1,0:T(8,128)} custom-call(s32[128]{0:T(128)} %cost_hbm.1, f32[8,128]{1,0:T(8,128)} %copy-done.10, f32[128,128]{1,0:T(8,128)} %mixing_hbm.1, s32[64,32]{1,0:T(8,128)} %copy-done.9, f32[128,128]{1,0:T(8,128)} %copy-done.3, f32[128,128]{1,0:T(8,128)} %copy-done.4, f32[256,128]{1,0:T(8,128)} %copy-done.5, f32[256,128]{1,0:T(8,128)} %copy-done.6, ...), custom_call_target="tpu_custom_call" | custom-call | flops 4294967296 | bytes 10485760 | tf_op jit(solution)/shard_map/mix/pallas_call | solution.py:658
  35.9 1.3 %all-to-all-done = f32[128,1,128]{2,1,0:T(1,128)S(1)} async-done(((f32[128,1,128]{2,1,0:T(1,128)}), f32[128,1,128]{2,1,0:T(1,128)S(1)}, u32[]{:S(2)}, u32[]{:S(2)}) %all-to-all-start) | async-done | bytes 65568 | tf_op jit(solution)/shard_map/all_to_all | solution.py:655
  37.2 1.0 %gather.1 = f32[16,128]{1,0:T(8,128)} custom-call(f32[128,128]{1,0:T(8,128)S(1)} %bitcast.11), custom_call_target="tpu_custom_call" | custom-call | flops 1048576 | bytes 1048576 | tf_op jit(solution)/shard_map/gather/pallas_call | solution.py:687
  (25 shorter events, 0.1 us)
Async XLA Ops:
  0.6 4.2 %copy-start = (f32[64,32,4,128]{3,2,1,0:T(4,128)S(1)}, f32[64,32,4,128]{3,2,1,0:T(4,128)}, u32[]{:S(2)}) copy-start(f32[64,32,4,128]{3,2,1,0:T(4,128)} %param.7) | copy-start | bytes 12582916
  0.6 4.2 %copy-start.1 = (f32[64,32,128]{2,1,0:T(8,128)S(1)}, f32[64,32,128]{2,1,0:T(8,128)}, u32[]{:S(2)}) copy-start(f32[64,32,128]{2,1,0:T(8,128)} %wx.1) | copy-start | bytes 3145732
  0.6 4.2 %copy-start.2 = (f32[64,32,128]{2,1,0:T(8,128)S(1)}, f32[64,32,128]{2,1,0:T(8,128)}, u32[]{:S(2)}) copy-start(f32[64,32,128]{2,1,0:T(8,128)} %wy.1) | copy-start | bytes 3145732
  2.0 11.1 %copy-start.14 = (s32[64,32]{0,1:T(8,128)S(1)}, s32[64,32]{0,1:T(8,128)}, u32[]{:S(2)}) copy-start(s32[64,32]{0,1:T(8,128)} %param.11) | copy-start | bytes 24580
  2.0 11.2 %copy-start.11 = (f32[128,128]{1,0:T(8,128)S(1)}, f32[128,128]{1,0:T(8,128)}, u32[]{:S(2)}) copy-start(f32[128,128]{1,0:T(8,128)} %mixing_hbm.1) | copy-start | bytes 196612
  2.1 11.2 %copy-start.12 = (s32[128]{0:T(128)S(1)}, s32[128]{0:T(128)}, u32[]{:S(2)}) copy-start(s32[128]{0:T(128)} %param.13) | copy-start | bytes 1540
  2.1 11.2 %copy-start.13 = (s32[128]{0:T(128)S(1)}, s32[128]{0:T(128)}, u32[]{:S(2)}) copy-start(s32[128]{0:T(128)} %cost_hbm.1) | copy-start | bytes 1540
  2.1 7.0 %collective-permute-start = (f32[128,128]{1,0:T(8,128)S(1)}, f32[128,128]{1,0:T(8,128)S(1)}, u32[]{:S(2)}, u32[]{:S(2)}) collective-permute-start(f32[128,128]{1,0:T(8,128)S(1)} %get-tuple-element.17), channel_id=1, source_target_pairs={{0,4},{4,0},{8,12},{12,8},{16,20},{20,16},{24,28},{28,24},{32,36},... | collective-permute-start | bytes 196616 | tf_op jit(solution)/shard_map/ppermute | solution.py:584
  3.6 5.5 %collective-permute-start.1 = (f32[128,128]{1,0:T(8,128)S(1)}, f32[128,128]{1,0:T(8,128)S(1)}, u32[]{:S(2)}, u32[]{:S(2)}) collective-permute-start(f32[128,128]{1,0:T(8,128)S(1)} %get-tuple-element.18), channel_id=1, source_target_pairs={{0,124},{4,8},{8,4},{12,16},{16,12},{20,24},{24,20},{28,32},{32,28... | collective-permute-start | bytes 196616 | tf_op jit(solution)/shard_map/ppermute | solution.py:583
  9.1 18.5 %copy-start.3 = (f32[128,128]{1,0:T(8,128)}, f32[128,128]{1,0:T(8,128)S(1)}, u32[]{:S(2)}) copy-start(f32[128,128]{1,0:T(8,128)S(1)} %collective-permute-done.got_a_ref.got_a_hbm) | copy-start | bytes 196612
  9.1 18.4 %copy-start.4 = (f32[128,128]{1,0:T(8,128)}, f32[128,128]{1,0:T(8,128)S(1)}, u32[]{:S(2)}) copy-start(f32[128,128]{1,0:T(8,128)S(1)} %collective-permute-done.1.got_b_ref.got_b_hbm) | copy-start | bytes 196612
  9.2 5.8 %collective-permute-start.2 = (f32[256,128]{1,0:T(8,128)S(1)}, f32[256,128]{1,0:T(8,128)S(1)}, u32[]{:S(2)}, u32[]{:S(2)}) collective-permute-start(f32[256,128]{1,0:T(8,128)S(1)} %get-tuple-element.20), channel_id=1, source_target_pairs={{0,1},{1,0},{2,3},{3,2},{4,5},{5,4},{6,7},{7,6},{8,9},{9,8},{10,11... | collective-permute-start | bytes 393224 | tf_op jit(solution)/shard_map/ppermute | solution.py:612
  10.9 5.0 %collective-permute-start.3 = (f32[256,128]{1,0:T(8,128)S(1)}, f32[256,128]{1,0:T(8,128)S(1)}, u32[]{:S(2)}, u32[]{:S(2)}) collective-permute-start(f32[256,128]{1,0:T(8,128)S(1)} %get-tuple-element.21), channel_id=1, source_target_pairs={{0,3},{1,2},{2,1},{3,0},{4,7},{5,6},{6,5},{7,4},{8,11},{9,10},{10,... | collective-permute-start | bytes 393224 | tf_op jit(solution)/shard_map/ppermute | solution.py:611
  13.2 14.3 %copy-start.9 = (s32[64,32]{1,0:T(8,128)}, s32[64,32]{1,0:T(8,128)S(1)}, u32[]{:S(2)}) copy-start(s32[64,32]{1,0:T(8,128)S(1)} %copy.11.trig_ref.trig_hbm) | copy-start | bytes 24580
  14.6 12.9 %copy-start.7 = (bf16[256,256]{1,0:T(8,128)(2,1)}, bf16[256,256]{1,0:T(8,128)(2,1)S(1)}, u32[]{:S(2)}) copy-start(bf16[256,256]{1,0:T(8,128)(2,1)S(1)} %get-tuple-element.22.first_hbm.first_ref) | copy-start | bytes 393220
  14.7 12.9 %copy-start.8 = (bf16[256,128]{1,0:T(8,128)(2,1)}, bf16[256,128]{1,0:T(8,128)(2,1)S(1)}, u32[]{:S(2)}) copy-start(bf16[256,128]{1,0:T(8,128)(2,1)S(1)} %get-tuple-element.23.second_hbm.second_ref) | copy-start | bytes 196612
  14.7 12.9 %copy-start.10 = (f32[8,128]{1,0:T(8,128)}, f32[8,128]{1,0:T(8,128)S(1)}, u32[]{:S(2)}) copy-start(f32[8,128]{1,0:T(8,128)S(1)} %get-tuple-element.16.bad_hbm.bad_ref) | copy-start | bytes 12292
  15.1 12.6 %copy-start.5 = (f32[256,128]{1,0:T(8,128)}, f32[256,128]{1,0:T(8,128)S(1)}, u32[]{:S(2)}) copy-start(f32[256,128]{1,0:T(8,128)S(1)} %collective-permute-done.2.got_c_hbm.got_c_ref) | copy-start | bytes 393220
  15.9 11.7 %copy-start.6 = (f32[256,128]{1,0:T(8,128)}, f32[256,128]{1,0:T(8,128)S(1)}, u32[]{:S(2)}) copy-start(f32[256,128]{1,0:T(8,128)S(1)} %collective-permute-done.3.got_d_hbm.got_d_ref) | copy-start | bytes 393220
  16.9 20.3 %all-to-all-start = ((f32[128,1,128]{2,1,0:T(1,128)}), f32[128,1,128]{2,1,0:T(1,128)S(1)}, u32[]{:S(2)}, u32[]{:S(2)}) async-start(f32[128,1,128]{2,1,0:T(1,128)} %bitcast.5), calls=%async_computation | async-start | bytes 131072 | tf_op jit(solution)/shard_map/all_to_all | solution.py:655

commit v3 on v2

--- a/solution.py
+++ b/solution.py
@@ -241,7 +241,6 @@
             edge_ref[x] = jnp.where(lower, v[0], v[-1])
             for i, value in enumerate(smooth_rows(v, None, None)):
                 adv[x, 8 * i:8 * i + 8, :] = state[x, 8 * i:8 * i + 8, :] + value
-            tracer_ref[x] = adv[x, pl.ds(1, rows // NT, stride=NT), :]
         out_copy(e).start()
 
     differentiate(0)
@@ -253,6 +252,8 @@
 
     lax.fori_loop(1, elements, step, 0)
     finish(elements - 1)
+    for x in range(elements * NP):
+        tracer_ref[x] = adv[x, pl.ds(1, rows // NT, stride=NT), :]
     for e in range(elements):
         out_copy(e).wait()
 

time: 38.4 us -> 38.3 us (level)
  no operation moved by 1% of the time
where the time goes in v3:
time: 38.3 us; the launch traced here: 38.2 us
  starting transfers between devices  17.6 us (46%)
  Pallas kernels  17.3 us (45%)
  waiting for transfers between devices  2.21 us (6%)
  between operations  0.9 us (2%)
    all_to_all x1, starting transfers between devices, body(): lax.all_to_all(outgoing, ('elem', 'blk'), split_axis=0, concat_axis=0, ti...  10.8 us
    pallas_call x1, Pallas kernels, body(): pl.pallas_call(mix_kernel, out_shape=struct(px, rows, lev), in_specs=[HBM...  8.23 us
    pallas_call x1, Pallas kernels, body(): pl.pallas_call(local_kernel, out_shape=(pltpu.HBM((px, rows, lev), F32),...  4.01 us
    ppermute x1, starting transfers between devices, body(): got_d = lax.ppermute(send_d, 'blk', pair_d)  2.24 us
    ppermute x1, starting transfers between devices, body(): got_c = lax.ppermute(send_c, 'blk', pair_c)  1.72 us
    ppermute x1, starting transfers between devices, body(): got_a = lax.ppermute(send_a, 'elem', pair_a)  1.5 us
    pallas_call x1, Pallas kernels, body(): pl.pallas_call(sides_kernel, out_shape=(struct(rows, lev),) * 2, in_specs...  1.37 us
    pallas_call x1, Pallas kernels, body(): pl.pallas_call(gains_kernel, out_shape=(struct(groups, lev), struct(2 * g...  1.36 us
  transfers between devices with their start and end apart: 5, of which 2 were waited for; matrix products, arithmetic and copies ran while one was open for 0% of the time, Pallas kernels for 37%

profile of v3, /device:TPU:1, one launch (start us, length us, event | category | flops | bytes accessed | tf_op | source)
XLA Modules:
  0.0 38.2 jit_solution(15916578057894652919)
XLA Ops:
  0.7 1.4 %sides.1 = (f32[128,128]{1,0:T(8,128)S(1)}, f32[128,128]{1,0:T(8,128)S(1)}) custom-call(f32[64,128,128]{2,1,0:T(8,128)} %bitcast.9, f32[64,32,128]{2,1,0:T(8,128)} %wx.1, f32[64,32,128]{2,1,0:T(8,128)} %wy.1), custom_call_target="tpu_custom_call" | custom-call | flops 2097152 | bytes 1048576 | tf_op jit(solution)/shard_map/sides/pallas_call | solution.py:563
  2.0 0.0 copy-start.14
  2.0 0.0 copy-start.11
  2.1 0.0 copy-start.12
  2.1 0.0 copy-start.13
  2.1 1.5 %collective-permute-start = (f32[128,128]{1,0:T(8,128)S(1)}, f32[128,128]{1,0:T(8,128)S(1)}, u32[]{:S(2)}, u32[]{:S(2)}) collective-permute-start(f32[128,128]{1,0:T(8,128)S(1)} %get-tuple-element.17), channel_id=1, source_target_pairs={{0,4},{4,0},{8,12},{12,8},{16,20},{20,16},{24,28},{28,24},{32,36},... | collective-permute-start | bytes 196616 | tf_op jit(solution)/shard_map/ppermute | solution.py:585
  3.6 1.3 %collective-permute-start.1 = (f32[128,128]{1,0:T(8,128)S(1)}, f32[128,128]{1,0:T(8,128)S(1)}, u32[]{:S(2)}, u32[]{:S(2)}) collective-permute-start(f32[128,128]{1,0:T(8,128)S(1)} %get-tuple-element.18), channel_id=1, source_target_pairs={{0,124},{4,8},{8,4},{12,16},{16,12},{20,24},{24,20},{28,32},{32,28... | collective-permute-start | bytes 196616 | tf_op jit(solution)/shard_map/ppermute | solution.py:584
  4.9 4.0 %local.1 = (f32[64,128,128]{2,1,0:T(8,128)}, f32[64,32,128]{2,1,0:T(8,128)S(1)}, f32[64,8,128]{2,1,0:T(8,128)S(1)}) custom-call(f32[64,128,128]{2,1,0:T(8,128)S(1)} %bitcast.10, f32[64,32,128]{2,1,0:T(8,128)S(1)} %copy-done.1, f32[64,32,128]{2,1,0:T(8,128)S(1)} %copy-done.2), custom_call_target="tpu_custom_call" | custom-call | flops 67108864 | bytes 12582912 | tf_op jit(solution)/shard_map/local/pallas_call | solution.py:587
  8.9 0.0 collective-permute-done.got_a_ref.got_a_hbm
  8.9 0.0 collective-permute-done.1.got_b_ref.got_b_hbm
  8.9 0.1 edges.1
  9.0 1.7 %collective-permute-start.2 = (f32[256,128]{1,0:T(8,128)S(1)}, f32[256,128]{1,0:T(8,128)S(1)}, u32[]{:S(2)}, u32[]{:S(2)}) collective-permute-start(f32[256,128]{1,0:T(8,128)S(1)} %get-tuple-element.20), channel_id=1, source_target_pairs={{0,1},{1,0},{2,3},{3,2},{4,5},{5,4},{6,7},{7,6},{8,9},{9,8},{10,11... | collective-permute-start | bytes 393224 | tf_op jit(solution)/shard_map/ppermute | solution.py:613
  10.7 2.2 %collective-permute-start.3 = (f32[256,128]{1,0:T(8,128)S(1)}, f32[256,128]{1,0:T(8,128)S(1)}, u32[]{:S(2)}, u32[]{:S(2)}) collective-permute-start(f32[256,128]{1,0:T(8,128)S(1)} %get-tuple-element.21), channel_id=1, source_target_pairs={{0,3},{1,2},{2,1},{3,0},{4,7},{5,6},{6,5},{7,4},{8,11},{9,10},{10,... | collective-permute-start | bytes 393224 | tf_op jit(solution)/shard_map/ppermute | solution.py:612
  13.0 0.1 copy.11.trig_ref.trig_hbm
  13.1 1.4 %gains.1 = (f32[128,128]{1,0:T(8,128)S(1)}, bf16[256,128]{1,0:T(8,128)(2,1)S(1)}, f32[128,128]{1,0:T(8,128)S(1)}, f32[128,128]{1,0:T(8,128)S(1)}, bf16[256,256]{...) custom-call(f32[128,128]{1,0:T(8,128)S(1)} %copy-done.11, s32[1,128]{1,0:T(1,128)S(1)} %bitcast.12, ...), custom_call_target="tpu_custom_call" | custom-call | flops 536870912 | bytes 1048576 | tf_op jit(solution)/shard_map/gains/pallas_call | solution.py:615
  14.5 0.0 copy-start.10
  14.5 0.4 early_rain.1.early_ref
  14.8 0.0 collective-permute-done.2.got_c_hbm.got_c_ref
  14.9 0.9 %collective-permute-done.3.got_d_hbm.got_d_ref = f32[256,128]{1,0:T(8,128)S(1)} collective-permute-done((f32[256,128]{1,0:T(8,128)S(1)}, f32[256,128]{1,0:T(8,128)S(1)}, u32[]{:S(2)}, u32[]{:S(2)}) %collective-permute-start.3) | collective-permute-done | bytes 131104 | tf_op jit(solution)/shard_map/ppermute | solution.py:612
  15.7 0.9 %rain.1 = f32[128,128]{1,0:T(8,128)} custom-call(f32[128,128]{1,0:T(8,128)S(1)} %get-tuple-element.25.costs_ref, f32[8,128]{1,0:T(8,128)S(1)} %get-tuple-element.16.bad_hbm.bad_ref, f32[64,32,128]{2,1,0:T(8,128)S(1)} %get-tuple-element.26.tracer_ref, f32[128,128]{1,0:T(8,128)S(1)} %collective-permute-done.got_a_ref.got_a_hbm, ...), custom_call_target="tpu_custom_call" | custom-call | flops 67108864 | bytes 2097152 | tf_op jit(solution)/shard_map/rain/pallas_call | solution.py:645
  16.7 10.8 %all-to-all-start = ((f32[128,1,128]{2,1,0:T(1,128)}), f32[128,1,128]{2,1,0:T(1,128)S(1)}, u32[]{:S(2)}, u32[]{:S(2)}) async-start(f32[128,1,128]{2,1,0:T(1,128)} %bitcast.5), calls=%async_computation | async-start | bytes 131072 | tf_op jit(solution)/shard_map/all_to_all | solution.py:656
  27.6 8.2 %mix.1 = f32[64,128,128]{2,1,0:T(8,128)} custom-call(s32[128]{0:T(128)} %cost_hbm.1, f32[8,128]{1,0:T(8,128)} %copy-done.10, f32[128,128]{1,0:T(8,128)} %mixing_hbm.1, s32[64,32]{1,0:T(8,128)} %copy-done.9, f32[128,128]{1,0:T(8,128)} %copy-done.3, f32[128,128]{1,0:T(8,128)} %copy-done.4, f32[256,128]{1,0:T(8,128)} %copy-done.5, f32[256,128]{1,0:T(8,128)} %copy-done.6, ...), custom_call_target="tpu_custom_call" | custom-call | flops 4294967296 | bytes 10485760 | tf_op jit(solution)/shard_map/mix/pallas_call | solution.py:659
  35.8 1.3 %all-to-all-done = f32[128,1,128]{2,1,0:T(1,128)S(1)} async-done(((f32[128,1,128]{2,1,0:T(1,128)}), f32[128,1,128]{2,1,0:T(1,128)S(1)}, u32[]{:S(2)}, u32[]{:S(2)}) %all-to-all-start) | async-done | bytes 65568 | tf_op jit(solution)/shard_map/all_to_all | solution.py:656
  37.2 1.0 %gather.1 = f32[16,128]{1,0:T(8,128)} custom-call(f32[128,128]{1,0:T(8,128)S(1)} %bitcast.11), custom_call_target="tpu_custom_call" | custom-call | flops 1048576 | bytes 1048576 | tf_op jit(solution)/shard_map/gather/pallas_call | solution.py:688
  (25 shorter events, 0.1 us)
Async XLA Ops:
  0.6 4.2 %copy-start = (f32[64,32,4,128]{3,2,1,0:T(4,128)S(1)}, f32[64,32,4,128]{3,2,1,0:T(4,128)}, u32[]{:S(2)}) copy-start(f32[64,32,4,128]{3,2,1,0:T(4,128)} %param.7) | copy-start | bytes 12582916
  0.6 4.2 %copy-start.1 = (f32[64,32,128]{2,1,0:T(8,128)S(1)}, f32[64,32,128]{2,1,0:T(8,128)}, u32[]{:S(2)}) copy-start(f32[64,32,128]{2,1,0:T(8,128)} %wx.1) | copy-start | bytes 3145732
  0.6 4.2 %copy-start.2 = (f32[64,32,128]{2,1,0:T(8,128)S(1)}, f32[64,32,128]{2,1,0:T(8,128)}, u32[]{:S(2)}) copy-start(f32[64,32,128]{2,1,0:T(8,128)} %wy.1) | copy-start | bytes 3145732
  2.0 10.9 %copy-start.14 = (s32[64,32]{0,1:T(8,128)S(1)}, s32[64,32]{0,1:T(8,128)}, u32[]{:S(2)}) copy-start(s32[64,32]{0,1:T(8,128)} %param.11) | copy-start | bytes 24580
  2.0 11.0 %copy-start.11 = (f32[128,128]{1,0:T(8,128)S(1)}, f32[128,128]{1,0:T(8,128)}, u32[]{:S(2)}) copy-start(f32[128,128]{1,0:T(8,128)} %mixing_hbm.1) | copy-start | bytes 196612
  2.1 11.0 %copy-start.12 = (s32[128]{0:T(128)S(1)}, s32[128]{0:T(128)}, u32[]{:S(2)}) copy-start(s32[128]{0:T(128)} %param.13) | copy-start | bytes 1540
  2.1 11.0 %copy-start.13 = (s32[128]{0:T(128)S(1)}, s32[128]{0:T(128)}, u32[]{:S(2)}) copy-start(s32[128]{0:T(128)} %cost_hbm.1) | copy-start | bytes 1540
  2.1 6.8 %collective-permute-start = (f32[128,128]{1,0:T(8,128)S(1)}, f32[128,128]{1,0:T(8,128)S(1)}, u32[]{:S(2)}, u32[]{:S(2)}) collective-permute-start(f32[128,128]{1,0:T(8,128)S(1)} %get-tuple-element.17), channel_id=1, source_target_pairs={{0,4},{4,0},{8,12},{12,8},{16,20},{20,16},{24,28},{28,24},{32,36},... | collective-permute-start | bytes 196616 | tf_op jit(solution)/shard_map/ppermute | solution.py:585
  3.6 5.3 %collective-permute-start.1 = (f32[128,128]{1,0:T(8,128)S(1)}, f32[128,128]{1,0:T(8,128)S(1)}, u32[]{:S(2)}, u32[]{:S(2)}) collective-permute-start(f32[128,128]{1,0:T(8,128)S(1)} %get-tuple-element.18), channel_id=1, source_target_pairs={{0,124},{4,8},{8,4},{12,16},{16,12},{20,24},{24,20},{28,32},{32,28... | collective-permute-start | bytes 196616 | tf_op jit(solution)/shard_map/ppermute | solution.py:584
  8.9 18.6 %copy-start.3 = (f32[128,128]{1,0:T(8,128)}, f32[128,128]{1,0:T(8,128)S(1)}, u32[]{:S(2)}) copy-start(f32[128,128]{1,0:T(8,128)S(1)} %collective-permute-done.got_a_ref.got_a_hbm) | copy-start | bytes 196612
  8.9 18.6 %copy-start.4 = (f32[128,128]{1,0:T(8,128)}, f32[128,128]{1,0:T(8,128)S(1)}, u32[]{:S(2)}) copy-start(f32[128,128]{1,0:T(8,128)S(1)} %collective-permute-done.1.got_b_ref.got_b_hbm) | copy-start | bytes 196612
  9.0 5.8 %collective-permute-start.2 = (f32[256,128]{1,0:T(8,128)S(1)}, f32[256,128]{1,0:T(8,128)S(1)}, u32[]{:S(2)}, u32[]{:S(2)}) collective-permute-start(f32[256,128]{1,0:T(8,128)S(1)} %get-tuple-element.20), channel_id=1, source_target_pairs={{0,1},{1,0},{2,3},{3,2},{4,5},{5,4},{6,7},{7,6},{8,9},{9,8},{10,11... | collective-permute-start | bytes 393224 | tf_op jit(solution)/shard_map/ppermute | solution.py:613
  10.7 5.0 %collective-permute-start.3 = (f32[256,128]{1,0:T(8,128)S(1)}, f32[256,128]{1,0:T(8,128)S(1)}, u32[]{:S(2)}, u32[]{:S(2)}) collective-permute-start(f32[256,128]{1,0:T(8,128)S(1)} %get-tuple-element.21), channel_id=1, source_target_pairs={{0,3},{1,2},{2,1},{3,0},{4,7},{5,6},{6,5},{7,4},{8,11},{9,10},{10,... | collective-permute-start | bytes 393224 | tf_op jit(solution)/shard_map/ppermute | solution.py:612
  13.0 14.5 %copy-start.9 = (s32[64,32]{1,0:T(8,128)}, s32[64,32]{1,0:T(8,128)S(1)}, u32[]{:S(2)}) copy-start(s32[64,32]{1,0:T(8,128)S(1)} %copy.11.trig_ref.trig_hbm) | copy-start | bytes 24580
  14.4 13.1 %copy-start.7 = (bf16[256,256]{1,0:T(8,128)(2,1)}, bf16[256,256]{1,0:T(8,128)(2,1)S(1)}, u32[]{:S(2)}) copy-start(bf16[256,256]{1,0:T(8,128)(2,1)S(1)} %get-tuple-element.22.first_hbm.first_ref) | copy-start | bytes 393220
  14.4 13.1 %copy-start.8 = (bf16[256,128]{1,0:T(8,128)(2,1)}, bf16[256,128]{1,0:T(8,128)(2,1)S(1)}, u32[]{:S(2)}) copy-start(bf16[256,128]{1,0:T(8,128)(2,1)S(1)} %get-tuple-element.23.second_hbm.second_ref) | copy-start | bytes 196612
  14.5 13.1 %copy-start.10 = (f32[8,128]{1,0:T(8,128)}, f32[8,128]{1,0:T(8,128)S(1)}, u32[]{:S(2)}) copy-start(f32[8,128]{1,0:T(8,128)S(1)} %get-tuple-element.16.bad_hbm.bad_ref) | copy-start | bytes 12292
  14.8 12.7 %copy-start.5 = (f32[256,128]{1,0:T(8,128)}, f32[256,128]{1,0:T(8,128)S(1)}, u32[]{:S(2)}) copy-start(f32[256,128]{1,0:T(8,128)S(1)} %collective-permute-done.2.got_c_hbm.got_c_ref) | copy-start | bytes 393220
  15.7 11.9 %copy-start.6 = (f32[256,128]{1,0:T(8,128)}, f32[256,128]{1,0:T(8,128)S(1)}, u32[]{:S(2)}) copy-start(f32[256,128]{1,0:T(8,128)S(1)} %collective-permute-done.3.got_d_hbm.got_d_ref) | copy-start | bytes 393220
  16.7 20.5 %all-to-all-start = ((f32[128,1,128]{2,1,0:T(1,128)}), f32[128,1,128]{2,1,0:T(1,128)S(1)}, u32[]{:S(2)}, u32[]{:S(2)}) async-start(f32[128,1,128]{2,1,0:T(1,128)} %bitcast.5), calls=%async_computation | async-start | bytes 131072 | tf_op jit(solution)/shard_map/all_to_all | solution.py:656

commit v4 on v3

--- a/solution.py
+++ b/solution.py
@@ -14,6 +14,7 @@
 GROUP_COLS = 16
 MAXC = 64
 LIMIT = 1.0e3
+HUGE = 3.38e38
 F32 = jnp.float32
 BF16 = jnp.bfloat16
 MIB = 1024 * 1024
@@ -172,21 +173,26 @@
     px = state_hbm.shape[0]
     copies = []
     for i, (element, x) in enumerate(((0, 0), (px - NP, px - 1))):
-        copies.append(pltpu.make_async_copy(state_hbm.at[pl.ds(element, NP)], state.at[i], sems.at[i]))
-        copies.append(pltpu.make_async_copy(wx_hbm.at[x], wx.at[i], sems.at[2 + i]))
-        copies.append(pltpu.make_async_copy(wy_hbm.at[x], wy.at[i], sems.at[4 + i]))
-    for copy in copies:
+        copies.append(
+            [
+                pltpu.make_async_copy(wx_hbm.at[x], wx.at[i], sems.at[2 + i]),
+                pltpu.make_async_copy(wy_hbm.at[x], wy.at[i], sems.at[4 + i]),
+                pltpu.make_async_copy(state_hbm.at[pl.ds(element, NP)], state.at[i], sems.at[i]),
+            ]
+        )
+    for copy in copies[0] + copies[1]:
         copy.start()
-    for copy in copies:
-        copy.wait()
-    for k in range(state.shape[2] // 16):
-        for s, at in ((0, 0), (1, NP - 1)):
-            def load(a, i):
-                return state[s, a, i:i + 8, :]
-
-            def store(a, i, value):
-                ends[s, i:i + 8, :] = value
-
+    for s, at in ((0, 0), (1, NP - 1)):
+        for copy in copies[s]:
+            copy.wait()
+
+        def load(a, i):
+            return state[s, a, i:i + 8, :]
+
+        def store(a, i, value):
+            ends[s, i:i + 8, :] = value
+
+        for k in range(state.shape[2] // 16):
             tendency(k, (at,), load, lambda a, y: wx[s, y:y + 1, :], lambda a, y: wy[s, y:y + 1, :], store)
     send_a_ref[...] = jnp.where(even, ends[1], ends[0])
     send_b_ref[...] = jnp.where(even, ends[0], ends[1])
@@ -327,7 +333,8 @@
     lane = iota((groups, LEV), 1)
 
     def send(rain):
-        values = jnp.where(lane == 2 * half, 1.0, jnp.where(lanes_ref[...] > 0.5, rain, 0.0))
+        rain = jnp.where(jnp.abs(rain) <= HUGE, rain, HUGE)
+        values = jnp.where(lane >= 2 * half, 1.0, jnp.where(lanes_ref[...] > 0.5, rain, 0.0))
         picked = exact_pick(onehot_ref[...], values)
         first, second = picked[:groups], picked[groups:]
         out_ref[...] = jnp.where(lane < half, first, jnp.where(lane < 2 * half, second, first + second))
@@ -513,10 +520,9 @@
     got = got_ref[...]
     size = got.shape
     half = GROUP_COLS
-    count_col = jnp.sum(jnp.where(iota(size, 1) == 2 * half, got, 0.0), axis=1, keepdims=True)
-    earlier = jnp.where(iota(size, 0) < iota(size, 1), count_col, 0.0)
-    start = jnp.sum(earlier, axis=0, keepdims=True).astype(jnp.int32)
-    count = jnp.sum(jnp.where(iota(size, 0) == iota(size, 1), count_col, 0.0), axis=0, keepdims=True).astype(jnp.int32)
+    counts = jnp.where(iota(size, 1) < 2 * half, pltpu.roll(got, LEV // 2, axis=1), got)
+    start = jnp.sum(jnp.where(iota(size, 0) < iota(size, 1), counts, 0.0), axis=0, keepdims=True).astype(jnp.int32)
+    count = jnp.sum(jnp.where(iota(size, 0) == iota(size, 1), counts, 0.0), axis=0, keepdims=True).astype(jnp.int32)
     per = LEV // half
     rows = size[0] // per
     slot = (iota(size, 0) % rows) * per + iota(size, 0) // rows

time: 38.3 us -> 38.3 us (level)
  no operation moved by 1% of the time
where the time goes in v4:
time: 38.3 us; the launch traced here: 38.2 us
  starting transfers between devices  17.6 us (46%)
  Pallas kernels  17.3 us (45%)
  waiting for transfers between devices  2.21 us (6%)
  between operations  0.9 us (2%)
    all_to_all x1, starting transfers between devices, body(): lax.all_to_all(outgoing, ('elem', 'blk'), split_axis=0, concat_axis=0, ti...  10.8 us
    pallas_call x1, Pallas kernels, body(): pl.pallas_call(mix_kernel, out_shape=struct(px, rows, lev), in_specs=[HBM...  8.23 us
    pallas_call x1, Pallas kernels, body(): pl.pallas_call(local_kernel, out_shape=(pltpu.HBM((px, rows, lev), F32),...  4.01 us
    ppermute x1, starting transfers between devices, body(): got_d = lax.ppermute(send_d, 'blk', pair_d)  2.24 us
    ppermute x1, starting transfers between devices, body(): got_c = lax.ppermute(send_c, 'blk', pair_c)  1.72 us
    ppermute x1, starting transfers between devices, body(): got_a = lax.ppermute(send_a, 'elem', pair_a)  1.5 us
    pallas_call x1, Pallas kernels, body(): pl.pallas_call(gains_kernel, out_shape=(struct(groups, lev), struct(2 * g...  1.36 us
    pallas_call x1, Pallas kernels, body(): pl.pallas_call(sides_kernel, out_shape=(struct(rows, lev),) * 2, in_specs...  1.35 us
  transfers between devices with their start and end apart: 5, of which 2 were waited for; matrix products, arithmetic and copies ran while one was open for 0% of the time, Pallas kernels for 37%

profile of v4, /device:TPU:1, one launch (start us, length us, event | category | flops | bytes accessed | tf_op | source)
XLA Modules:
  0.0 38.2 jit_solution(10268322391919650141)
XLA Ops:
  0.7 1.4 %sides.1 = (f32[128,128]{1,0:T(8,128)S(1)}, f32[128,128]{1,0:T(8,128)S(1)}) custom-call(f32[64,128,128]{2,1,0:T(8,128)} %bitcast.9, f32[64,32,128]{2,1,0:T(8,128)} %wx.1, f32[64,32,128]{2,1,0:T(8,128)} %wy.1), custom_call_target="tpu_custom_call" | custom-call | flops 2097152 | bytes 1048576 | tf_op jit(solution)/shard_map/sides/pallas_call | solution.py:569
  2.0 0.0 copy-start.14
  2.0 0.0 copy-start.11
  2.0 0.0 copy-start.12
  2.1 0.0 copy-start.13
  2.1 1.5 %collective-permute-start = (f32[128,128]{1,0:T(8,128)S(1)}, f32[128,128]{1,0:T(8,128)S(1)}, u32[]{:S(2)}, u32[]{:S(2)}) collective-permute-start(f32[128,128]{1,0:T(8,128)S(1)} %get-tuple-element.17), channel_id=1, source_target_pairs={{0,4},{4,0},{8,12},{12,8},{16,20},{20,16},{24,28},{28,24},{32,36},... | collective-permute-start | bytes 196616 | tf_op jit(solution)/shard_map/ppermute | solution.py:591
  3.6 1.3 %collective-permute-start.1 = (f32[128,128]{1,0:T(8,128)S(1)}, f32[128,128]{1,0:T(8,128)S(1)}, u32[]{:S(2)}, u32[]{:S(2)}) collective-permute-start(f32[128,128]{1,0:T(8,128)S(1)} %get-tuple-element.18), channel_id=1, source_target_pairs={{0,124},{4,8},{8,4},{12,16},{16,12},{20,24},{24,20},{28,32},{32,28... | collective-permute-start | bytes 196616 | tf_op jit(solution)/shard_map/ppermute | solution.py:590
  4.8 4.0 %local.1 = (f32[64,128,128]{2,1,0:T(8,128)}, f32[64,32,128]{2,1,0:T(8,128)S(1)}, f32[64,8,128]{2,1,0:T(8,128)S(1)}) custom-call(f32[64,128,128]{2,1,0:T(8,128)S(1)} %bitcast.10, f32[64,32,128]{2,1,0:T(8,128)S(1)} %copy-done.1, f32[64,32,128]{2,1,0:T(8,128)S(1)} %copy-done.2), custom_call_target="tpu_custom_call" | custom-call | flops 67108864 | bytes 12582912 | tf_op jit(solution)/shard_map/local/pallas_call | solution.py:593
  8.9 0.0 collective-permute-done.got_a_ref.got_a_hbm
  8.9 0.0 collective-permute-done.1.got_b_ref.got_b_hbm
  8.9 0.1 edges.1
  9.0 1.7 %collective-permute-start.2 = (f32[256,128]{1,0:T(8,128)S(1)}, f32[256,128]{1,0:T(8,128)S(1)}, u32[]{:S(2)}, u32[]{:S(2)}) collective-permute-start(f32[256,128]{1,0:T(8,128)S(1)} %get-tuple-element.20), channel_id=1, source_target_pairs={{0,1},{1,0},{2,3},{3,2},{4,5},{5,4},{6,7},{7,6},{8,9},{9,8},{10,11... | collective-permute-start | bytes 393224 | tf_op jit(solution)/shard_map/ppermute | solution.py:619
  10.7 2.2 %collective-permute-start.3 = (f32[256,128]{1,0:T(8,128)S(1)}, f32[256,128]{1,0:T(8,128)S(1)}, u32[]{:S(2)}, u32[]{:S(2)}) collective-permute-start(f32[256,128]{1,0:T(8,128)S(1)} %get-tuple-element.21), channel_id=1, source_target_pairs={{0,3},{1,2},{2,1},{3,0},{4,7},{5,6},{6,5},{7,4},{8,11},{9,10},{10,... | collective-permute-start | bytes 393224 | tf_op jit(solution)/shard_map/ppermute | solution.py:618
  12.9 0.1 copy.11.trig_ref.trig_hbm
  13.1 1.4 %gains.1 = (f32[128,128]{1,0:T(8,128)S(1)}, bf16[256,128]{1,0:T(8,128)(2,1)S(1)}, f32[128,128]{1,0:T(8,128)S(1)}, f32[128,128]{1,0:T(8,128)S(1)}, bf16[256,256]{...) custom-call(f32[128,128]{1,0:T(8,128)S(1)} %copy-done.11, s32[1,128]{1,0:T(1,128)S(1)} %bitcast.12, ...), custom_call_target="tpu_custom_call" | custom-call | flops 536870912 | bytes 1048576 | tf_op jit(solution)/shard_map/gains/pallas_call | solution.py:621
  14.4 0.0 copy-start.10
  14.5 0.4 early_rain.1.early_ref
  14.8 0.0 collective-permute-done.2.got_c_hbm.got_c_ref
  14.8 0.9 %collective-permute-done.3.got_d_hbm.got_d_ref = f32[256,128]{1,0:T(8,128)S(1)} collective-permute-done((f32[256,128]{1,0:T(8,128)S(1)}, f32[256,128]{1,0:T(8,128)S(1)}, u32[]{:S(2)}, u32[]{:S(2)}) %collective-permute-start.3) | collective-permute-done | bytes 131104 | tf_op jit(solution)/shard_map/ppermute | solution.py:618
  15.7 0.9 %rain.1 = f32[128,128]{1,0:T(8,128)} custom-call(f32[128,128]{1,0:T(8,128)S(1)} %get-tuple-element.25.costs_ref, f32[8,128]{1,0:T(8,128)S(1)} %get-tuple-element.16.bad_hbm.bad_ref, f32[64,32,128]{2,1,0:T(8,128)S(1)} %get-tuple-element.26.tracer_ref, f32[128,128]{1,0:T(8,128)S(1)} %collective-permute-done.got_a_ref.got_a_hbm, ...), custom_call_target="tpu_custom_call" | custom-call | flops 67108864 | bytes 2097152 | tf_op jit(solution)/shard_map/rain/pallas_call | solution.py:651
  16.7 10.8 %all-to-all-start = ((f32[128,1,128]{2,1,0:T(1,128)}), f32[128,1,128]{2,1,0:T(1,128)S(1)}, u32[]{:S(2)}, u32[]{:S(2)}) async-start(f32[128,1,128]{2,1,0:T(1,128)} %bitcast.5), calls=%async_computation | async-start | bytes 131072 | tf_op jit(solution)/shard_map/all_to_all | solution.py:662
  27.6 8.2 %mix.1 = f32[64,128,128]{2,1,0:T(8,128)} custom-call(s32[128]{0:T(128)} %cost_hbm.1, f32[8,128]{1,0:T(8,128)} %copy-done.10, f32[128,128]{1,0:T(8,128)} %mixing_hbm.1, s32[64,32]{1,0:T(8,128)} %copy-done.9, f32[128,128]{1,0:T(8,128)} %copy-done.3, f32[128,128]{1,0:T(8,128)} %copy-done.4, f32[256,128]{1,0:T(8,128)} %copy-done.5, f32[256,128]{1,0:T(8,128)} %copy-done.6, ...), custom_call_target="tpu_custom_call" | custom-call | flops 4294967296 | bytes 10485760 | tf_op jit(solution)/shard_map/mix/pallas_call | solution.py:665
  35.8 1.3 %all-to-all-done = f32[128,1,128]{2,1,0:T(1,128)S(1)} async-done(((f32[128,1,128]{2,1,0:T(1,128)}), f32[128,1,128]{2,1,0:T(1,128)S(1)}, u32[]{:S(2)}, u32[]{:S(2)}) %all-to-all-start) | async-done | bytes 65568 | tf_op jit(solution)/shard_map/all_to_all | solution.py:662
  37.2 1.0 %gather.1 = f32[16,128]{1,0:T(8,128)} custom-call(f32[128,128]{1,0:T(8,128)S(1)} %bitcast.11), custom_call_target="tpu_custom_call" | custom-call | flops 1048576 | bytes 1048576 | tf_op jit(solution)/shard_map/gather/pallas_call | solution.py:694
  (25 shorter events, 0.1 us)
Async XLA Ops:
  0.6 4.2 %copy-start = (f32[64,32,4,128]{3,2,1,0:T(4,128)S(1)}, f32[64,32,4,128]{3,2,1,0:T(4,128)}, u32[]{:S(2)}) copy-start(f32[64,32,4,128]{3,2,1,0:T(4,128)} %param.7) | copy-start | bytes 12582916
  0.6 4.2 %copy-start.1 = (f32[64,32,128]{2,1,0:T(8,128)S(1)}, f32[64,32,128]{2,1,0:T(8,128)}, u32[]{:S(2)}) copy-start(f32[64,32,128]{2,1,0:T(8,128)} %wx.1) | copy-start | bytes 3145732
  0.6 4.2 %copy-start.2 = (f32[64,32,128]{2,1,0:T(8,128)S(1)}, f32[64,32,128]{2,1,0:T(8,128)}, u32[]{:S(2)}) copy-start(f32[64,32,128]{2,1,0:T(8,128)} %wy.1) | copy-start | bytes 3145732
  2.0 10.9 %copy-start.14 = (s32[64,32]{0,1:T(8,128)S(1)}, s32[64,32]{0,1:T(8,128)}, u32[]{:S(2)}) copy-start(s32[64,32]{0,1:T(8,128)} %param.11) | copy-start | bytes 24580
  2.0 11.0 %copy-start.11 = (f32[128,128]{1,0:T(8,128)S(1)}, f32[128,128]{1,0:T(8,128)}, u32[]{:S(2)}) copy-start(f32[128,128]{1,0:T(8,128)} %mixing_hbm.1) | copy-start | bytes 196612
  2.0 11.0 %copy-start.12 = (s32[128]{0:T(128)S(1)}, s32[128]{0:T(128)}, u32[]{:S(2)}) copy-start(s32[128]{0:T(128)} %param.13) | copy-start | bytes 1540
  2.1 11.0 %copy-start.13 = (s32[128]{0:T(128)S(1)}, s32[128]{0:T(128)}, u32[]{:S(2)}) copy-start(s32[128]{0:T(128)} %cost_hbm.1) | copy-start | bytes 1540
  2.1 6.8 %collective-permute-start = (f32[128,128]{1,0:T(8,128)S(1)}, f32[128,128]{1,0:T(8,128)S(1)}, u32[]{:S(2)}, u32[]{:S(2)}) collective-permute-start(f32[128,128]{1,0:T(8,128)S(1)} %get-tuple-element.17), channel_id=1, source_target_pairs={{0,4},{4,0},{8,12},{12,8},{16,20},{20,16},{24,28},{28,24},{32,36},... | collective-permute-start | bytes 196616 | tf_op jit(solution)/shard_map/ppermute | solution.py:591
  3.6 5.3 %collective-permute-start.1 = (f32[128,128]{1,0:T(8,128)S(1)}, f32[128,128]{1,0:T(8,128)S(1)}, u32[]{:S(2)}, u32[]{:S(2)}) collective-permute-start(f32[128,128]{1,0:T(8,128)S(1)} %get-tuple-element.18), channel_id=1, source_target_pairs={{0,124},{4,8},{8,4},{12,16},{16,12},{20,24},{24,20},{28,32},{32,28... | collective-permute-start | bytes 196616 | tf_op jit(solution)/shard_map/ppermute | solution.py:590
  8.9 18.6 %copy-start.3 = (f32[128,128]{1,0:T(8,128)}, f32[128,128]{1,0:T(8,128)S(1)}, u32[]{:S(2)}) copy-start(f32[128,128]{1,0:T(8,128)S(1)} %collective-permute-done.got_a_ref.got_a_hbm) | copy-start | bytes 196612
  8.9 18.6 %copy-start.4 = (f32[128,128]{1,0:T(8,128)}, f32[128,128]{1,0:T(8,128)S(1)}, u32[]{:S(2)}) copy-start(f32[128,128]{1,0:T(8,128)S(1)} %collective-permute-done.1.got_b_ref.got_b_hbm) | copy-start | bytes 196612
  9.0 5.8 %collective-permute-start.2 = (f32[256,128]{1,0:T(8,128)S(1)}, f32[256,128]{1,0:T(8,128)S(1)}, u32[]{:S(2)}, u32[]{:S(2)}) collective-permute-start(f32[256,128]{1,0:T(8,128)S(1)} %get-tuple-element.20), channel_id=1, source_target_pairs={{0,1},{1,0},{2,3},{3,2},{4,5},{5,4},{6,7},{7,6},{8,9},{9,8},{10,11... | collective-permute-start | bytes 393224 | tf_op jit(solution)/shard_map/ppermute | solution.py:619
  10.7 5.0 %collective-permute-start.3 = (f32[256,128]{1,0:T(8,128)S(1)}, f32[256,128]{1,0:T(8,128)S(1)}, u32[]{:S(2)}, u32[]{:S(2)}) collective-permute-start(f32[256,128]{1,0:T(8,128)S(1)} %get-tuple-element.21), channel_id=1, source_target_pairs={{0,3},{1,2},{2,1},{3,0},{4,7},{5,6},{6,5},{7,4},{8,11},{9,10},{10,... | collective-permute-start | bytes 393224 | tf_op jit(solution)/shard_map/ppermute | solution.py:618
  13.0 14.5 %copy-start.9 = (s32[64,32]{1,0:T(8,128)}, s32[64,32]{1,0:T(8,128)S(1)}, u32[]{:S(2)}) copy-start(s32[64,32]{1,0:T(8,128)S(1)} %copy.11.trig_ref.trig_hbm) | copy-start | bytes 24580
  14.4 13.1 %copy-start.7 = (bf16[256,256]{1,0:T(8,128)(2,1)}, bf16[256,256]{1,0:T(8,128)(2,1)S(1)}, u32[]{:S(2)}) copy-start(bf16[256,256]{1,0:T(8,128)(2,1)S(1)} %get-tuple-element.22.first_hbm.first_ref) | copy-start | bytes 393220
  14.4 13.1 %copy-start.8 = (bf16[256,128]{1,0:T(8,128)(2,1)}, bf16[256,128]{1,0:T(8,128)(2,1)S(1)}, u32[]{:S(2)}) copy-start(bf16[256,128]{1,0:T(8,128)(2,1)S(1)} %get-tuple-element.23.second_hbm.second_ref) | copy-start | bytes 196612
  14.4 13.1 %copy-start.10 = (f32[8,128]{1,0:T(8,128)}, f32[8,128]{1,0:T(8,128)S(1)}, u32[]{:S(2)}) copy-start(f32[8,128]{1,0:T(8,128)S(1)} %get-tuple-element.16.bad_hbm.bad_ref) | copy-start | bytes 12292
  14.8 12.7 %copy-start.5 = (f32[256,128]{1,0:T(8,128)}, f32[256,128]{1,0:T(8,128)S(1)}, u32[]{:S(2)}) copy-start(f32[256,128]{1,0:T(8,128)S(1)} %collective-permute-done.2.got_c_hbm.got_c_ref) | copy-start | bytes 393220
  15.7 11.9 %copy-start.6 = (f32[256,128]{1,0:T(8,128)}, f32[256,128]{1,0:T(8,128)S(1)}, u32[]{:S(2)}) copy-start(f32[256,128]{1,0:T(8,128)S(1)} %collective-permute-done.3.got_d_hbm.got_d_ref) | copy-start | bytes 393220
  16.7 20.5 %all-to-all-start = ((f32[128,1,128]{2,1,0:T(1,128)}), f32[128,1,128]{2,1,0:T(1,128)S(1)}, u32[]{:S(2)}, u32[]{:S(2)}) async-start(f32[128,1,128]{2,1,0:T(1,128)} %bitcast.5), calls=%async_computation | async-start | bytes 131072 | tf_op jit(solution)/shard_map/all_to_all | solution.py:662

commit v5 on v4

--- a/solution.py
+++ b/solution.py
@@ -177,11 +177,11 @@
             [
                 pltpu.make_async_copy(wx_hbm.at[x], wx.at[i], sems.at[2 + i]),
                 pltpu.make_async_copy(wy_hbm.at[x], wy.at[i], sems.at[4 + i]),
-                pltpu.make_async_copy(state_hbm.at[pl.ds(element, NP)], state.at[i], sems.at[i]),
             ]
+            + [pltpu.make_async_copy(state_hbm.at[element + a], state.at[i, a], sems.at[6 + NP * i + a]) for a in range(NP)]
         )
     for copy in copies[0] + copies[1]:
-        copy.start()
+        copy.start(priority=1)
     for s, at in ((0, 0), (1, NP - 1)):
         for copy in copies[s]:
             copy.wait()
@@ -576,7 +576,7 @@
             pltpu.VMEM((2, py, lev), F32),
             pltpu.VMEM((2, py, lev), F32),
             pltpu.VMEM((2, rows, lev), F32),
-            pltpu.SemaphoreType.DMA((6,)),
+            pltpu.SemaphoreType.DMA((6 + 2 * NP,)),
         ],
         compiler_params=params(4),
         cost_estimate=cost(2 * MIB, MIB),

time: 38.3 us -> 38.4 us (level)
  no operation moved by 1% of the time
where the time goes in v5:
time: 38.4 us; the launch traced here: 38.2 us
  starting transfers between devices  17.6 us (46%)
  Pallas kernels  17.4 us (45%)
  waiting for transfers between devices  2.21 us (6%)
  between operations  0.9 us (2%)
    all_to_all x1, starting transfers between devices, body(): lax.all_to_all(outgoing, ('elem', 'blk'), split_axis=0, concat_axis=0, ti...  10.8 us
    pallas_call x1, Pallas kernels, body(): pl.pallas_call(mix_kernel, out_shape=struct(px, rows, lev), in_specs=[HBM...  8.23 us
    pallas_call x1, Pallas kernels, body(): pl.pallas_call(local_kernel, out_shape=(pltpu.HBM((px, rows, lev), F32),...  4.01 us
    ppermute x1, starting transfers between devices, body(): got_d = lax.ppermute(send_d, 'blk', pair_d)  2.24 us
    ppermute x1, starting transfers between devices, body(): got_c = lax.ppermute(send_c, 'blk', pair_c)  1.72 us
    ppermute x1, starting transfers between devices, body(): got_a = lax.ppermute(send_a, 'elem', pair_a)  1.5 us
    pallas_call x1, Pallas kernels, body(): pl.pallas_call(sides_kernel, out_shape=(struct(rows, lev),) * 2, in_specs...  1.43 us
    pallas_call x1, Pallas kernels, body(): pl.pallas_call(gains_kernel, out_shape=(struct(groups, lev), struct(2 * g...  1.36 us
  transfers between devices with their start and end apart: 5, of which 2 were waited for; matrix products, arithmetic and copies ran while one was open for 0% of the time, Pallas kernels for 37%

profile of v5, /device:TPU:1, one launch (start us, length us, event | category | flops | bytes accessed | tf_op | source)
XLA Modules:
  0.0 38.2 jit_solution(13320599539864284128)
XLA Ops:
  0.7 1.4 %sides.1 = (f32[128,128]{1,0:T(8,128)S(1)}, f32[128,128]{1,0:T(8,128)S(1)}) custom-call(f32[64,128,128]{2,1,0:T(8,128)} %bitcast.9, f32[64,32,128]{2,1,0:T(8,128)} %wx.1, f32[64,32,128]{2,1,0:T(8,128)} %wy.1), custom_call_target="tpu_custom_call" | custom-call | flops 2097152 | bytes 1048576 | tf_op jit(solution)/shard_map/sides/pallas_call | solution.py:569
  2.1 0.0 copy-start.14
  2.1 0.0 copy-start.11
  2.1 0.0 copy-start.12
  2.1 0.0 copy-start.13
  2.1 1.5 %collective-permute-start = (f32[128,128]{1,0:T(8,128)S(1)}, f32[128,128]{1,0:T(8,128)S(1)}, u32[]{:S(2)}, u32[]{:S(2)}) collective-permute-start(f32[128,128]{1,0:T(8,128)S(1)} %get-tuple-element.17), channel_id=1, source_target_pairs={{0,4},{4,0},{8,12},{12,8},{16,20},{20,16},{24,28},{28,24},{32,36},... | collective-permute-start | bytes 196616 | tf_op jit(solution)/shard_map/ppermute | solution.py:591
  3.6 1.3 %collective-permute-start.1 = (f32[128,128]{1,0:T(8,128)S(1)}, f32[128,128]{1,0:T(8,128)S(1)}, u32[]{:S(2)}, u32[]{:S(2)}) collective-permute-start(f32[128,128]{1,0:T(8,128)S(1)} %get-tuple-element.18), channel_id=1, source_target_pairs={{0,124},{4,8},{8,4},{12,16},{16,12},{20,24},{24,20},{28,32},{32,28... | collective-permute-start | bytes 196616 | tf_op jit(solution)/shard_map/ppermute | solution.py:590
  4.9 4.0 %local.1 = (f32[64,128,128]{2,1,0:T(8,128)}, f32[64,32,128]{2,1,0:T(8,128)S(1)}, f32[64,8,128]{2,1,0:T(8,128)S(1)}) custom-call(f32[64,128,128]{2,1,0:T(8,128)S(1)} %bitcast.10, f32[64,32,128]{2,1,0:T(8,128)S(1)} %copy-done.1, f32[64,32,128]{2,1,0:T(8,128)S(1)} %copy-done.2), custom_call_target="tpu_custom_call" | custom-call | flops 67108864 | bytes 12582912 | tf_op jit(solution)/shard_map/local/pallas_call | solution.py:593
  8.9 0.0 collective-permute-done.got_a_ref.got_a_hbm
  9.0 0.0 collective-permute-done.1.got_b_ref.got_b_hbm
  9.0 0.1 edges.1
  9.1 1.7 %collective-permute-start.2 = (f32[256,128]{1,0:T(8,128)S(1)}, f32[256,128]{1,0:T(8,128)S(1)}, u32[]{:S(2)}, u32[]{:S(2)}) collective-permute-start(f32[256,128]{1,0:T(8,128)S(1)} %get-tuple-element.20), channel_id=1, source_target_pairs={{0,1},{1,0},{2,3},{3,2},{4,5},{5,4},{6,7},{7,6},{8,9},{9,8},{10,11... | collective-permute-start | bytes 393224 | tf_op jit(solution)/shard_map/ppermute | solution.py:619
  10.8 2.2 %collective-permute-start.3 = (f32[256,128]{1,0:T(8,128)S(1)}, f32[256,128]{1,0:T(8,128)S(1)}, u32[]{:S(2)}, u32[]{:S(2)}) collective-permute-start(f32[256,128]{1,0:T(8,128)S(1)} %get-tuple-element.21), channel_id=1, source_target_pairs={{0,3},{1,2},{2,1},{3,0},{4,7},{5,6},{6,5},{7,4},{8,11},{9,10},{10,... | collective-permute-start | bytes 393224 | tf_op jit(solution)/shard_map/ppermute | solution.py:618
  13.0 0.1 copy.11.trig_ref.trig_hbm
  13.1 1.4 %gains.1 = (f32[128,128]{1,0:T(8,128)S(1)}, bf16[256,128]{1,0:T(8,128)(2,1)S(1)}, f32[128,128]{1,0:T(8,128)S(1)}, f32[128,128]{1,0:T(8,128)S(1)}, bf16[256,256]{...) custom-call(f32[128,128]{1,0:T(8,128)S(1)} %copy-done.11, s32[1,128]{1,0:T(1,128)S(1)} %bitcast.12, ...), custom_call_target="tpu_custom_call" | custom-call | flops 536870912 | bytes 1048576 | tf_op jit(solution)/shard_map/gains/pallas_call | solution.py:621
  14.5 0.0 copy-start.10
  14.5 0.4 early_rain.1.early_ref
  14.9 0.0 collective-permute-done.2.got_c_hbm.got_c_ref
  14.9 0.9 %collective-permute-done.3.got_d_hbm.got_d_ref = f32[256,128]{1,0:T(8,128)S(1)} collective-permute-done((f32[256,128]{1,0:T(8,128)S(1)}, f32[256,128]{1,0:T(8,128)S(1)}, u32[]{:S(2)}, u32[]{:S(2)}) %collective-permute-start.3) | collective-permute-done | bytes 131104 | tf_op jit(solution)/shard_map/ppermute | solution.py:618
  15.8 0.9 %rain.1 = f32[128,128]{1,0:T(8,128)} custom-call(f32[128,128]{1,0:T(8,128)S(1)} %get-tuple-element.25.costs_ref, f32[8,128]{1,0:T(8,128)S(1)} %get-tuple-element.16.bad_hbm.bad_ref, f32[64,32,128]{2,1,0:T(8,128)S(1)} %get-tuple-element.26.tracer_ref, f32[128,128]{1,0:T(8,128)S(1)} %collective-permute-done.got_a_ref.got_a_hbm, ...), custom_call_target="tpu_custom_call" | custom-call | flops 67108864 | bytes 2097152 | tf_op jit(solution)/shard_map/rain/pallas_call | solution.py:651
  16.7 10.8 %all-to-all-start = ((f32[128,1,128]{2,1,0:T(1,128)}), f32[128,1,128]{2,1,0:T(1,128)S(1)}, u32[]{:S(2)}, u32[]{:S(2)}) async-start(f32[128,1,128]{2,1,0:T(1,128)} %bitcast.5), calls=%async_computation | async-start | bytes 131072 | tf_op jit(solution)/shard_map/all_to_all | solution.py:662
  27.7 8.2 %mix.1 = f32[64,128,128]{2,1,0:T(8,128)} custom-call(s32[128]{0:T(128)} %cost_hbm.1, f32[8,128]{1,0:T(8,128)} %copy-done.10, f32[128,128]{1,0:T(8,128)} %mixing_hbm.1, s32[64,32]{1,0:T(8,128)} %copy-done.9, f32[128,128]{1,0:T(8,128)} %copy-done.3, f32[128,128]{1,0:T(8,128)} %copy-done.4, f32[256,128]{1,0:T(8,128)} %copy-done.5, f32[256,128]{1,0:T(8,128)} %copy-done.6, ...), custom_call_target="tpu_custom_call" | custom-call | flops 4294967296 | bytes 10485760 | tf_op jit(solution)/shard_map/mix/pallas_call | solution.py:665
  35.9 1.3 %all-to-all-done = f32[128,1,128]{2,1,0:T(1,128)S(1)} async-done(((f32[128,1,128]{2,1,0:T(1,128)}), f32[128,1,128]{2,1,0:T(1,128)S(1)}, u32[]{:S(2)}, u32[]{:S(2)}) %all-to-all-start) | async-done | bytes 65568 | tf_op jit(solution)/shard_map/all_to_all | solution.py:662
  37.2 1.0 %gather.1 = f32[16,128]{1,0:T(8,128)} custom-call(f32[128,128]{1,0:T(8,128)S(1)} %bitcast.11), custom_call_target="tpu_custom_call" | custom-call | flops 1048576 | bytes 1048576 | tf_op jit(solution)/shard_map/gather/pallas_call | solution.py:694
  (25 shorter events, 0.1 us)
Async XLA Ops:
  0.6 4.3 %copy-start = (f32[64,32,4,128]{3,2,1,0:T(4,128)S(1)}, f32[64,32,4,128]{3,2,1,0:T(4,128)}, u32[]{:S(2)}) copy-start(f32[64,32,4,128]{3,2,1,0:T(4,128)} %param.7) | copy-start | bytes 12582916
  0.6 4.3 %copy-start.1 = (f32[64,32,128]{2,1,0:T(8,128)S(1)}, f32[64,32,128]{2,1,0:T(8,128)}, u32[]{:S(2)}) copy-start(f32[64,32,128]{2,1,0:T(8,128)} %wx.1) | copy-start | bytes 3145732
  0.6 4.3 %copy-start.2 = (f32[64,32,128]{2,1,0:T(8,128)S(1)}, f32[64,32,128]{2,1,0:T(8,128)}, u32[]{:S(2)}) copy-start(f32[64,32,128]{2,1,0:T(8,128)} %wy.1) | copy-start | bytes 3145732
  2.1 10.9 %copy-start.14 = (s32[64,32]{0,1:T(8,128)S(1)}, s32[64,32]{0,1:T(8,128)}, u32[]{:S(2)}) copy-start(s32[64,32]{0,1:T(8,128)} %param.11) | copy-start | bytes 24580
  2.1 11.0 %copy-start.11 = (f32[128,128]{1,0:T(8,128)S(1)}, f32[128,128]{1,0:T(8,128)}, u32[]{:S(2)}) copy-start(f32[128,128]{1,0:T(8,128)} %mixing_hbm.1) | copy-start | bytes 196612
  2.1 11.0 %copy-start.12 = (s32[128]{0:T(128)S(1)}, s32[128]{0:T(128)}, u32[]{:S(2)}) copy-start(s32[128]{0:T(128)} %param.13) | copy-start | bytes 1540
  2.1 11.0 %copy-start.13 = (s32[128]{0:T(128)S(1)}, s32[128]{0:T(128)}, u32[]{:S(2)}) copy-start(s32[128]{0:T(128)} %cost_hbm.1) | copy-start | bytes 1540
  2.1 6.8 %collective-permute-start = (f32[128,128]{1,0:T(8,128)S(1)}, f32[128,128]{1,0:T(8,128)S(1)}, u32[]{:S(2)}, u32[]{:S(2)}) collective-permute-start(f32[128,128]{1,0:T(8,128)S(1)} %get-tuple-element.17), channel_id=1, source_target_pairs={{0,4},{4,0},{8,12},{12,8},{16,20},{20,16},{24,28},{28,24},{32,36},... | collective-permute-start | bytes 196616 | tf_op jit(solution)/shard_map/ppermute | solution.py:591
  3.6 5.3 %collective-permute-start.1 = (f32[128,128]{1,0:T(8,128)S(1)}, f32[128,128]{1,0:T(8,128)S(1)}, u32[]{:S(2)}, u32[]{:S(2)}) collective-permute-start(f32[128,128]{1,0:T(8,128)S(1)} %get-tuple-element.18), channel_id=1, source_target_pairs={{0,124},{4,8},{8,4},{12,16},{16,12},{20,24},{24,20},{28,32},{32,28... | collective-permute-start | bytes 196616 | tf_op jit(solution)/shard_map/ppermute | solution.py:590
  9.0 18.6 %copy-start.3 = (f32[128,128]{1,0:T(8,128)}, f32[128,128]{1,0:T(8,128)S(1)}, u32[]{:S(2)}) copy-start(f32[128,128]{1,0:T(8,128)S(1)} %collective-permute-done.got_a_ref.got_a_hbm) | copy-start | bytes 196612
  9.0 18.6 %copy-start.4 = (f32[128,128]{1,0:T(8,128)}, f32[128,128]{1,0:T(8,128)S(1)}, u32[]{:S(2)}) copy-start(f32[128,128]{1,0:T(8,128)S(1)} %collective-permute-done.1.got_b_ref.got_b_hbm) | copy-start | bytes 196612
  9.1 5.8 %collective-permute-start.2 = (f32[256,128]{1,0:T(8,128)S(1)}, f32[256,128]{1,0:T(8,128)S(1)}, u32[]{:S(2)}, u32[]{:S(2)}) collective-permute-start(f32[256,128]{1,0:T(8,128)S(1)} %get-tuple-element.20), channel_id=1, source_target_pairs={{0,1},{1,0},{2,3},{3,2},{4,5},{5,4},{6,7},{7,6},{8,9},{9,8},{10,11... | collective-permute-start | bytes 393224 | tf_op jit(solution)/shard_map/ppermute | solution.py:619
  10.8 5.0 %collective-permute-start.3 = (f32[256,128]{1,0:T(8,128)S(1)}, f32[256,128]{1,0:T(8,128)S(1)}, u32[]{:S(2)}, u32[]{:S(2)}) collective-permute-start(f32[256,128]{1,0:T(8,128)S(1)} %get-tuple-element.21), channel_id=1, source_target_pairs={{0,3},{1,2},{2,1},{3,0},{4,7},{5,6},{6,5},{7,4},{8,11},{9,10},{10,... | collective-permute-start | bytes 393224 | tf_op jit(solution)/shard_map/ppermute | solution.py:618
  13.1 14.5 %copy-start.9 = (s32[64,32]{1,0:T(8,128)}, s32[64,32]{1,0:T(8,128)S(1)}, u32[]{:S(2)}) copy-start(s32[64,32]{1,0:T(8,128)S(1)} %copy.11.trig_ref.trig_hbm) | copy-start | bytes 24580
  14.5 13.1 %copy-start.7 = (bf16[256,256]{1,0:T(8,128)(2,1)}, bf16[256,256]{1,0:T(8,128)(2,1)S(1)}, u32[]{:S(2)}) copy-start(bf16[256,256]{1,0:T(8,128)(2,1)S(1)} %get-tuple-element.22.first_hbm.first_ref) | copy-start | bytes 393220
  14.5 13.1 %copy-start.8 = (bf16[256,128]{1,0:T(8,128)(2,1)}, bf16[256,128]{1,0:T(8,128)(2,1)S(1)}, u32[]{:S(2)}) copy-start(bf16[256,128]{1,0:T(8,128)(2,1)S(1)} %get-tuple-element.23.second_hbm.second_ref) | copy-start | bytes 196612
  14.5 13.1 %copy-start.10 = (f32[8,128]{1,0:T(8,128)}, f32[8,128]{1,0:T(8,128)S(1)}, u32[]{:S(2)}) copy-start(f32[8,128]{1,0:T(8,128)S(1)} %get-tuple-element.16.bad_hbm.bad_ref) | copy-start | bytes 12292
  14.9 12.7 %copy-start.5 = (f32[256,128]{1,0:T(8,128)}, f32[256,128]{1,0:T(8,128)S(1)}, u32[]{:S(2)}) copy-start(f32[256,128]{1,0:T(8,128)S(1)} %collective-permute-done.2.got_c_hbm.got_c_ref) | copy-start | bytes 393220
  15.8 11.9 %copy-start.6 = (f32[256,128]{1,0:T(8,128)}, f32[256,128]{1,0:T(8,128)S(1)}, u32[]{:S(2)}) copy-start(f32[256,128]{1,0:T(8,128)S(1)} %collective-permute-done.3.got_d_hbm.got_d_ref) | copy-start | bytes 393220
  16.7 20.5 %all-to-all-start = ((f32[128,1,128]{2,1,0:T(1,128)}), f32[128,1,128]{2,1,0:T(1,128)S(1)}, u32[]{:S(2)}, u32[]{:S(2)}) async-start(f32[128,1,128]{2,1,0:T(1,128)} %bitcast.5), calls=%async_computation | async-start | bytes 131072 | tf_op jit(solution)/shard_map/all_to_all | solution.py:662
